TPU v7x, 32 devices: a whole 2x2x4 slice. The times are simulated.
32 devices in a mesh: dp: 16 (over z, y, x), seq: 2 (over core).
Axes of the slice: x: 2, y: 2, z: 4, core: 2. Of those that a mesh axis runs over, the one named last changes fastest.
Arguments:
- latents: float32 [16, 512, 1024], P('dp', 'seq'), may hold values from -6 to 6
- pixels: float32 [16, 8192, 261], P('dp', 'seq'), may hold values from -6 to 6
- keep_mask: int32 [16, 8192], P('dp', 'seq'), may hold values from 0 to 1, as said below
- cotangent: float32 [16, 512, 1024], P('dp', 'seq'), may hold values from -6 to 6
- square_weights: float32 [4, 1024, 1024], P(None, None, 'dp')
- square_first: float32 [4, 1024, 1024], P(None, None, 'dp')
- square_second: float32 [4, 1024, 1024], P(None, None, 'dp')
- pixel_weights: float32 [2, 261, 1024], P(None, None, 'dp')
- pixel_first: float32 [2, 261, 1024], P(None, None, 'dp')
- pixel_second: float32 [2, 261, 1024], P(None, None, 'dp')
- latent_vectors: float32 [6, 1024], replicated
- latent_first: float32 [6, 1024], replicated
- latent_second: float32 [6, 1024], replicated
- pixel_norm: float32 [2, 261], replicated
- pixel_norm_first: float32 [2, 261], replicated
- pixel_norm_second: float32 [2, 261], replicated
Outputs:
- latents_out: float32 [16, 512, 1024], P('dp', 'seq')
- latents_grad: float32 [16, 512, 1024], P('dp', 'seq')
- pixels_grad: float32 [16, 8192, 261], P('dp', 'seq')
- square_grad: float32 [4, 1024, 1024], P(None, None, 'dp')
- square_first_new: float32 [4, 1024, 1024], P(None, None, 'dp')
- square_second_new: float32 [4, 1024, 1024], P(None, None, 'dp')
- square_new: float32 [4, 1024, 1024], P(None, None, 'dp')
- square_half: bfloat16 [4, 1024, 1024], P(None, None, 'dp')
- pixel_weight_grad: float32 [2, 261, 1024], P(None, None, 'dp')
- pixel_first_new: float32 [2, 261, 1024], P(None, None, 'dp')
- pixel_second_new: float32 [2, 261, 1024], P(None, None, 'dp')
- pixel_new: float32 [2, 261, 1024], P(None, None, 'dp')
- pixel_half: bfloat16 [2, 261, 1024], P(None, None, 'dp')
- latent_first_new: float32 [6, 1024], replicated
- latent_second_new: float32 [6, 1024], replicated
- latent_vectors_new: float32 [6, 1024], replicated
- pixel_norm_first_new: float32 [2, 261], replicated
- pixel_norm_second_new: float32 [2, 261], replicated
- pixel_norm_new: float32 [2, 261], replicated
- matrix_norms: float32 [3, 6], replicated
Inputs may be any that keep to these rules, and one draw needn't show every extreme that they name: keep_mask[i, 0] = 1 for every image i; each image drops its other pixels with a share drawn for it between 10 and 60 percent.
All inputs are finite; a program needn't handle non-finite values.
Results may differ from a plain program's by a relative error of at most 0.015.
The roundings to bfloat16 on the way count: a program that leaves them out, or rounds other values in their place, can miss the bound.
Values may be sent and summed in bfloat16 or wider, within the bound.
No kernel may reach another device: no remote copies, remote signals or barrier semaphores. Data moves between devices by JAX's collectives and lax.ppermute only.
A program may use at most 320 MiB of HBM per device.

v0:
```python
import functools

import jax
import jax.numpy as jnp
from jax import lax
from jax.experimental import pallas as pl
from jax.experimental.pallas import tpu as pltpu
from jax.sharding import PartitionSpec as P

STEP = 10


norm_epsilon = 1e-05
beta_one = 0.9
beta_two = 0.999
decay_rate = 0.01
epsilon = 1e-06
learn_rate = 0.25
vector_rate = 1.0
masked_score = -1e30
gelu_coeff = 0.7978845608028654


def adam_moments(grad, first, second):
    first_new = beta_one * first + (1.0 - beta_one) * grad
    second_new = beta_two * second + (1.0 - beta_two) * grad * grad
    ratio = (
        first_new
        / (1.0 - beta_one**STEP)
        / (jnp.sqrt(second_new / (1.0 - beta_two**STEP)) + epsilon)
    )
    return (first_new, second_new, ratio)

half = jnp.bfloat16
single = jnp.float32
swap = [(0, 1), (1, 0)]
main, rest = 256, 128
whole = pl.BlockSpec(memory_space=pltpu.VMEM)
remote = pl.BlockSpec(memory_space=pl.ANY)
scalars = pl.BlockSpec(memory_space=pltpu.SMEM)
params = pltpu.CompilerParams(vmem_limit_bytes=40 * 2**20)
params_most = pltpu.CompilerParams(vmem_limit_bytes=56 * 2**20)
params_all = pltpu.CompilerParams(vmem_limit_bytes=63 * 2**20)


def cost(micros):
    return pl.CostEstimate(flops=int(micros * 1.1e9), bytes_accessed=1024, transcendentals=0)


def shape(dims, dtype):
    return jax.ShapeDtypeStruct(dims, dtype)


def contract(left, right, over_left, over_right):
    return lax.dot_general(left, right, (((over_left,), (over_right,)), ((), ())), preferred_element_type=single)


def nn(left, right):
    return contract(left, right, 1, 0)


def nt(left, right):
    return contract(left, right, 1, 1)


def tn(left, right):
    return contract(left, right, 0, 0)


def flip(array, mask):
    return lax.ppermute(array, "dp", [(i, i ^ mask) for i in range(lax.axis_size("dp"))])


def trade(array):
    return lax.ppermute(array, "seq", swap)


def special(groups, shard):
    return groups == 16 and shard % 32 == 0


def tie_kernel(*refs):
    pass


def tie(arrays, *after):
    return pl.pallas_call(
        tie_kernel,
        out_shape=[shape(a.shape, a.dtype) for a in arrays],
        in_specs=[remote] * (len(arrays) + len(after)),
        out_specs=[remote] * len(arrays),
        input_output_aliases={i: i for i in range(len(arrays))},
        cost_estimate=cost(0.1),
        name="tie",
    )(*arrays, *after)


def stack_kernel(plan, *refs):
    outs = refs[len(refs) - len(plan) :]
    for out, parts in zip(outs, plan):
        rows = out.shape[0] // len(parts)
        for i, (source, part) in enumerate(parts):
            out[pl.ds(i * rows, rows), :] = refs[source][pl.ds(part * rows, rows), :]


def stack(arrays, rows, plan, *after):
    lanes, dtype = arrays[0].shape[1], arrays[0].dtype
    return pl.pallas_call(
        functools.partial(stack_kernel, plan),
        out_shape=[shape((rows * len(parts), lanes), dtype) for parts in plan],
        in_specs=[whole] * len(arrays) + [remote] * len(after),
        out_specs=[whole] * len(plan),
        compiler_params=params,
        cost_estimate=cost(1.5),
        name="stack",
    )(*arrays, *after)


def gather_blocks(block, early, late):
    rows = block.shape[0]
    one, two, four, three, eight = [flip(block, o) for o in (1, 2, 4, 3, 8)]
    across, both = stack([three, four, eight], rows, (((0, 0), (2, 0)), ((1, 0), (2, 0))), early)
    (gathered,) = stack([block, eight, four, three, two, one], rows, (tuple((i, 0) for i in range(6)),))
    second = [flip(across, 4), flip(both, 2), flip(both, 1)]
    seven, twelve, twelve_ten = stack(second[:2], rows, (((0, 0),), ((0, 1),), ((0, 1), (1, 1))), second[2], late)
    third = [flip(seven, 8), flip(twelve, 2), flip(twelve_ten, 1)]
    return [
        ((0, 8, 4, 3, 2, 1), gathered),
        ((7, 12), second[0]),
        ((6, 10), second[1]),
        ((5, 9), second[2]),
        ((15,), third[0]),
        ((14,), third[1]),
        ((13, 11), third[2]),
    ]


def pack_kernel(feats, spot, squares, pixels, block):
    side = spot[1]
    part = squares.shape[2] // 2
    lanes = pl.ds(pl.multiple_of(side * part, part), part)
    over = feats - main

    def pixel(m):
        last = pixels[m, :, pl.ds(main, over)]
        last = jnp.concatenate([last, jnp.zeros((last.shape[0], main - over), single)], axis=1)
        return jnp.where(side == 0, pixels[m, :, pl.ds(0, main)], last).astype(half)

    block[:, pl.ds(0, part)] = squares[0, :, lanes].astype(half)
    block[:, pl.ds(part, main)] = pixel(0)
    block[:, pl.ds(part + main, main)] = pixel(1)
    for m in range(1, 4):
        block[:, pl.ds(m * part + 2 * main, part)] = squares[m, :, lanes].astype(half)


def pack(spot, squares, pixels):
    _, shard, width = squares.shape
    return pl.pallas_call(
        functools.partial(pack_kernel, pixels.shape[2]),
        out_shape=shape((shard, 4 * (width // 2) + 2 * main), half),
        in_specs=[scalars, whole, whole],
        out_specs=whole,
        compiler_params=params,
        cost_estimate=cost(2),
        name="pack",
    )(spot, squares, pixels)


def gather_matrices(block, early, late):
    groups = lax.axis_size("dp")
    shard = block.shape[0]
    if special(groups, shard):
        arrays, layout = [], []
        for positions, array in gather_blocks(block, early, late):
            arrays += [array, trade(array)]
            layout += [(positions, 0), (positions, 1)]
        return arrays, tuple(layout)
    every = lax.all_gather(block, ("dp", "seq"), axis=0).reshape(groups, 2, shard, -1)
    return [every.transpose(1, 0, 2, 3).reshape(2, groups * shard, -1)], ()


def place_blocks(spot, blocks, layout, target, first):
    lanes = pl.ds(first, target.shape[2])
    if not layout:
        target[...] = blocks[0][:, :, lanes]
    for block, (positions, turn) in zip(blocks, layout):
        rows = block.shape[0] // len(positions)
        side = lax.bitwise_xor(spot[1], turn)
        for i, o in enumerate(positions):
            chip = lax.bitwise_xor(spot[0], o)
            place = pl.ds(pl.multiple_of(chip * rows, rows), rows)
            target[side, place, :] = block[pl.ds(i * rows, rows), lanes]


def copy_all(pairs, sems, first=0):
    copies = [pltpu.make_async_copy(source, target, sems.at[first + i]) for i, (source, target) in enumerate(pairs)]
    for copy in copies:
        copy.start()
    return copies


def wait_all(copies):
    for copy in copies:
        copy.wait()


def load_blocks(spot, blocks, layout, target, first, sems, base=0):
    pairs = []
    lanes = pl.ds(first, target.shape[2])
    if not layout:
        pairs.append((blocks[0].at[:, :, lanes], target))
    for block, (positions, turn) in zip(blocks, layout):
        rows = block.shape[0] // len(positions)
        side = lax.bitwise_xor(spot[1], turn)
        for i, o in enumerate(positions):
            chip = lax.bitwise_xor(spot[0], o)
            place = target.at[side, pl.ds(pl.multiple_of(chip * rows, rows), rows)]
            pairs.append((block.at[pl.ds(i * rows, rows), lanes], place))
    return copy_all(pairs, sems, base)


written = ((13, 11), (14,), (15,), (5, 9), (6, 10), (7, 12), (1,), (2,), (3,), (4,), (8,), (0,))


def store_terms(spot, terms, outs, start, count, sems, base):
    lanes = pl.ds(start, count)
    if len(outs) == 1:
        return copy_all([(terms.at[:, lanes], outs[0].at[:, lanes])], sems, base)
    pairs = []
    rows = terms.shape[0] // 16
    for positions, out in zip(written, outs):
        for i, o in enumerate(positions):
            chip = lax.bitwise_xor(spot[0], o)
            source = terms.at[pl.ds(pl.multiple_of(chip * rows, rows), rows), lanes]
            pairs.append((source, out.at[pl.ds(i * rows, rows), lanes]))
    return copy_all(pairs, sems, base)


def term_shapes(groups, shard, lanes):
    if special(groups, shard):
        return [shape((len(positions) * shard, lanes), half) for positions in written]
    return [shape((groups * shard, lanes), half)]


def send_first(terms, *after):
    if len(terms) == 1:
        return None
    got = [flip(terms[0], 1), flip(terms[1], 2), flip(terms[2], 8)]
    return tie(got, *after) if after else got


def send_second(terms, got, *after):
    if len(terms) == 1:
        return None
    rows = terms[-1].shape[0]

    def added(array, low, *high):
        total = array.astype(single)
        if low is not None:
            total = total + jnp.pad(low.astype(single), ((0, rows), (0, 0)))
        for other in high:
            total = total + jnp.pad(other.astype(single), ((rows, 0), (0, 0)))
        return total.astype(half)

    twelve, ten = got[0][:rows], got[0][rows:]
    got = [
        flip(terms[3], 1),
        flip(added(terms[4], None, ten), 2),
        flip(added(terms[5], got[2], twelve, got[1]), 4),
    ]
    return tie(got, *after) if after else got


def send_third(terms, got):
    if len(terms) == 1:
        return [lax.psum_scatter(terms[0], "dp", scatter_dimension=0, tiled=True)]
    rows = terms[-1].shape[0]
    one, two = terms[6:8]
    three, four, eight = [term.astype(single) for term in terms[8:11]]
    upper = [array[:rows].astype(single) for array in got]
    lower = [array[rows:].astype(single) for array in got]
    sent = [
        (one, 1),
        (two, 2),
        (four + upper[0] + upper[1], 4),
        (three + upper[2], 3),
        (eight + lower[0] + lower[1] + lower[2], 8),
    ]
    return [flip(array.astype(half), mask) for array, mask in sent]


def sum_own(terms, got):
    if len(terms) > 1:
        got = [terms[-1], *got]
    total = got[0].astype(single)
    for array in got[1:]:
        total = total + array.astype(single)
    return total


def sum_all(array):
    mask = 1
    size = lax.axis_size("dp")
    while mask < size:
        if mask * 2 < size:
            one, two, three = flip(array, mask), flip(array, 2 * mask), flip(array, 3 * mask)
            array = (array + one) + (two + three)
            mask *= 4
        else:
            array = array + flip(array, mask)
            mask *= 2
    return array


def standard(values):
    center = values - jnp.mean(values, axis=-1, keepdims=True)
    inverse = lax.rsqrt(jnp.mean(center * center, axis=-1, keepdims=True) + norm_epsilon)
    return center * inverse, inverse


def standard_back(grad, gain, unit, inverse):
    scaled = grad * gain
    return inverse * (
        scaled - jnp.mean(scaled, axis=-1, keepdims=True) - unit * jnp.mean(scaled * unit, axis=-1, keepdims=True)
    )


def pixel_kernel(pixels, gain, shift, normed, stats, held, tail, sem):
    copy = pltpu.make_async_copy(pixels.at[:, 0, :], held, sem)
    copy.start()
    feats = held.shape[0]
    step = 256
    over = feats - main
    tail[...] = jnp.zeros_like(tail)
    copy.wait()

    @pl.loop(0, held.shape[1] // step)
    def _(i):
        lanes = pl.ds(pl.multiple_of(i * step, step), step)
        first, last = held[pl.ds(0, main), lanes], held[pl.ds(main, over), lanes]
        mean = (jnp.sum(first, axis=0, keepdims=True) + jnp.sum(last, axis=0, keepdims=True)) / feats
        first, last = first - mean, last - mean
        spread = (
            jnp.sum(first * first, axis=0, keepdims=True) + jnp.sum(last * last, axis=0, keepdims=True)
        ) / feats
        inverse = lax.rsqrt(spread + norm_epsilon)
        normed[pl.ds(0, main), lanes] = (first * inverse * gain[pl.ds(0, main)] + shift[pl.ds(0, main)]).astype(half)
        tail[pl.ds(0, over), :] = last * inverse * gain[pl.ds(main, over)] + shift[pl.ds(main, over)]
        normed[pl.ds(main, rest), lanes] = tail[...].astype(half)
        stats[0:1, lanes] = mean
        stats[1:2, lanes] = inverse


def norm_pixels(pixels, gain, shift):
    feats, _, count = pixels.shape
    return pl.pallas_call(
        pixel_kernel,
        out_shape=[shape((main + rest, count), half), shape((2, count), single)],
        in_specs=[remote, whole, whole],
        out_specs=[whole] * 2,
        scratch_shapes=[pltpu.VMEM((feats, count), single), pltpu.VMEM((rest, 256), single), pltpu.SemaphoreType.DMA],
        compiler_params=params,
        cost_estimate=cost(7),
        name="norm_pixels",
    )(pixels, gain, shift)


def latent_kernel(latents, vectors, normed):
    unit, _ = standard(latents[...])
    normed[...] = (unit * vectors[0:1, :] + vectors[1:2, :]).astype(half)


def norm_latents(latents, vectors):
    return pl.pallas_call(
        latent_kernel,
        out_shape=shape(latents.shape, half),
        in_specs=[whole] * 2,
        out_specs=whole,
        compiler_params=params,
        cost_estimate=cost(2),
        name="norm_latents",
    )(latents, vectors)


def attend_kernel(count, layout, scale, feats, spot, *refs):
    blocks = refs[:count]
    mine, theirs, pixels_in, keep, query_out, query_pix, sent, *refs = refs[count:]
    weights, normed, pixels, query, scores, peak, more = refs
    copies = copy_all([(mine, normed.at[0]), (theirs, normed.at[1])], more)
    late = copy_all([(pixels_in, pixels)], more, 2)
    place_blocks(spot, blocks, layout, weights, 0)
    wait_all(copies)
    step, part = mine.shape[0], mine.shape[1] // 2
    for t in range(2):
        rows = pl.ds(t * step, step)
        value = nt(normed[t, :, pl.ds(0, part)], weights[0, :, pl.ds(0, part)])
        value = value + nt(normed[t, :, pl.ds(part, part)], weights[1, :, pl.ds(0, part)])
        value = value.astype(half)
        query[rows, :] = value
        query_pix[rows, pl.ds(0, main)] = (nn(value, weights[0, :, pl.ds(part, main)]) * scale).astype(half)
        query_pix[rows, pl.ds(main, rest)] = (nn(value, weights[1, :, pl.ds(part, rest)]) * scale).astype(half)
    wait_all(late)
    late = copy_all([(query, query_out)], more, 2)
    step = 1024
    peak[...] = jnp.full(peak.shape, -jnp.inf, single)

    @pl.loop(0, pixels.shape[1] // step)
    def _(j):
        lanes = pl.ds(pl.multiple_of(j * step, step), step)
        value = nn(query_pix[...], pixels[:, lanes])
        value = jnp.where(keep[:, lanes] > 0, value, masked_score)
        scores[:, lanes] = value
        some = [value[:, 128 * k : 128 * k + 128] for k in range(step // 128)]
        peak[...] = functools.reduce(jnp.maximum, some, peak[...])

    top = jnp.max(peak[...], axis=-1, keepdims=True)
    peak[...] = jnp.zeros_like(peak)
    sent[...] = jnp.zeros_like(sent)

    @pl.loop(0, pixels.shape[1] // step)
    def _(j):
        lanes = pl.ds(pl.multiple_of(j * step, step), step)
        value = jnp.exp(scores[:, lanes] - top)
        peak[...] += sum(value[:, 128 * k : 128 * k + 128] for k in range(step // 128))
        sent[...] += nt(value.astype(half), pixels[:, lanes])

    total, mix = peak[...], sent[...]
    total = jnp.sum(total, axis=-1, keepdims=True)
    lane = lax.broadcasted_iota(jnp.int32, mix.shape, 1)
    sent[...] = jnp.where(lane == feats, top, jnp.where(lane == feats + 1, total, mix))
    wait_all(late)


def attend(spot, gathered, normed, pixels, keep, scale, feats):
    blocks, layout = gathered
    rows, width = 2 * normed[0].shape[0], normed[0].shape[1]
    lanes = width // 2 + main
    return pl.pallas_call(
        functools.partial(attend_kernel, len(blocks), layout, scale, feats),
        out_shape=[shape((rows, width), half), shape((rows, main + rest), half), shape((rows, main + rest), single)],
        in_specs=[scalars] + [whole] * len(blocks) + [remote] * 3 + [whole],
        out_specs=[remote, whole, whole],
        scratch_shapes=[
            pltpu.VMEM((2, width, lanes), half),
            pltpu.VMEM((2, rows // 2, width), half),
            pltpu.VMEM(pixels.shape, half),
            pltpu.VMEM((rows, width), half),
            pltpu.VMEM((rows, pixels.shape[1]), single),
            pltpu.VMEM((rows, 128), single),
            pltpu.SemaphoreType.DMA((3,)),
        ],
        compiler_params=params,
        cost_estimate=cost(11),
        name="attend",
    )(spot, *blocks, *normed, pixels, keep)


def chain_kernel(count, layout, terms_count, feats, spot, *refs):
    blocks, refs = refs[:count], refs[count:]
    mine, theirs, latent_mine, latent_theirs, cot_mine, cot_theirs, vectors, *refs = refs
    latents_out, middle_grad, grad_pix, stats, sums, *refs = refs
    term_outs, refs = refs[:terms_count], refs[terms_count:]
    near, far, latents_in, cot_in, mixes, *refs = refs
    attended, middle_half, mixed, hidden_grad, active, out_half, attended_grad, value_mix, *refs = refs
    wide, out_wide, grad_wide, scratch, terms, sems, store_sems, more = refs
    rows_all, width = attended.shape
    step = rows_all // 2
    part = width // 2
    ready = copy_all([(mine, mixes.at[0]), (theirs, mixes.at[1])], more)
    ready += load_blocks(spot, blocks, layout, near, part + main, sems)
    ready_latents = copy_all([(latent_mine, latents_in.at[0]), (latent_theirs, latents_in.at[1])], more, 2)
    matrices = ((near, main), (far, 0), (far, part))
    leaving = []
    pair = range(2)
    rows = [pl.ds(t * step, step) for t in pair]

    def into(value, m):
        source, start = matrices[m]
        lanes = pl.ds(start, part)
        return nt(value[:, :part], source[0, :, lanes]) + nt(value[:, part:], source[1, :, lanes])

    def back(value, m, target):
        source, start = matrices[m]
        lanes = pl.ds(start, part)
        target[:, pl.ds(0, part)] = nn(value, source[0, :, lanes])
        target[:, pl.ds(part, part)] = nn(value, source[1, :, lanes])

    side = pl.ds(pl.multiple_of(spot[1] * part, part), part)

    def term(m, grad, value):
        terms[:, pl.ds(m * part, part)] = tn(grad[...], value[:, side]).astype(half)
        return store_terms(spot, terms, term_outs, m * part, part, store_sems, 16 * m)

    sums[...] = jnp.zeros_like(sums)
    value_mix[...] = jnp.zeros_like(value_mix)
    wait_all(ready)
    ready_far = load_blocks(spot, blocks, layout, far, 2 * part + 2 * main, sems, 32)
    ready_far += copy_all([(cot_mine, cot_in.at[0]), (cot_theirs, cot_in.at[1])], more, 4)
    tops, totals, attended_f, middles, units, inverses, hiddens, curves = [[None, None] for _ in range(8)]
    for t in pair:
        here, there = mixes[0, rows[t], :], mixes[1, rows[1 - t], :]
        top_here, top_there = here[:, feats : feats + 1], there[:, feats : feats + 1]
        top = jnp.maximum(top_here, top_there)
        scale_here, scale_there = jnp.exp(top_here - top), jnp.exp(top_there - top)
        total = here[:, feats + 1 : feats + 2] * scale_here + there[:, feats + 1 : feats + 2] * scale_there
        mix = (here * scale_here + there * scale_there) / total
        lane = lax.broadcasted_iota(jnp.int32, mix.shape, 1)
        value_mix[rows[t], pl.ds(0, main + rest)] = jnp.where(lane < feats, mix, 0.0).astype(half)
        tops[t], totals[t] = top, total
    for t in pair:
        value = nt(value_mix[rows[t], pl.ds(0, main)], near[0, :, pl.ds(0, main)])
        value = value + nt(value_mix[rows[t], pl.ds(main, rest)], near[1, :, pl.ds(0, rest)])
        wide[t] = value
        attended[rows[t], :] = value.astype(half)
    wait_all(ready_latents)
    for t in pair:
        middles[t] = latents_in[t] + into(attended[rows[t], :], 0)
    for t in pair:
        units[t], inverses[t] = standard(middles[t])
        mixed[rows[t], :] = (units[t] * vectors[2:3, :] + vectors[3:4, :]).astype(half)
    wait_all(ready_far)
    for t in pair:
        value = cot_in[t].astype(half)
        out_half[rows[t], :] = value
        if t == 0:
            sums[5:6, :] = jnp.sum(value.astype(single), axis=0, keepdims=True)
    for t in pair:
        hiddens[t] = into(mixed[rows[t], :], 1) + vectors[4:5, :]
    for t in pair:
        back(out_half[rows[t], :], 2, scratch.at[t])
        hidden = hiddens[t]
        curve = jnp.tanh(gelu_coeff * (hidden + 0.044715 * hidden * hidden * hidden))
        active[rows[t], :] = (0.5 * hidden * (1.0 + curve)).astype(half)
        curves[t] = curve
    leaving += term(2, out_half, active)
    out_wide[...] = middles[0] + into(active[rows[0], :], 2) + vectors[5:6, :]
    leaving += copy_all([(out_wide, latents_out)], more)
    for t in pair:
        hidden, curve = hiddens[t], curves[t]
        slope = 0.5 * (1.0 + curve) + 0.5 * hidden * (1.0 - curve * curve) * gelu_coeff * (
            1.0 + 3.0 * 0.044715 * hidden * hidden
        )
        value = (scratch[t] * slope).astype(half)
        hidden_grad[rows[t], :] = value
        if t == 0:
            sums[4:5, :] = jnp.sum(value.astype(single), axis=0, keepdims=True)
    for t in pair:
        back(hidden_grad[rows[t], :], 1, scratch.at[t])
    leaving += term(1, hidden_grad, mixed)
    for t in pair:
        mixed_grad = scratch[t]
        if t == 0:
            sums[2:3, :] = jnp.sum(mixed_grad * units[t], axis=0, keepdims=True)
            sums[3:4, :] = jnp.sum(mixed_grad, axis=0, keepdims=True)
        grad = cot_in[t] + standard_back(mixed_grad, vectors[2:3, :], units[t], inverses[t])
        if t == 0:
            grad_wide[...] = grad
            leaving += copy_all([(grad_wide, middle_grad)], more, 1)
        middle_half[rows[t], :] = grad.astype(half)
    for t in pair:
        back(middle_half[rows[t], :], 0, scratch.at[t])
    leaving += term(0, middle_half, attended)
    for t in pair:
        value = scratch[t].astype(half)
        attended_grad[rows[t], :] = value
        inner = jnp.sum(wide[t] * value.astype(single), axis=-1, keepdims=True)
        lane = lax.broadcasted_iota(jnp.int32, (step, 128), 1)
        stats[rows[t], :] = jnp.where(lane == 0, tops[t] + jnp.log(totals[t]), inner)
    for t in pair:
        value = attended_grad[rows[t], :]
        grad_pix[rows[t], pl.ds(0, main)] = nn(value, near[0, :, pl.ds(0, main)]).astype(half)
        grad_pix[rows[t], pl.ds(main, rest)] = nn(value, near[1, :, pl.ds(0, rest)]).astype(half)
    side = pl.ds(pl.multiple_of(spot[1] * main, main), main)
    terms[:, pl.ds(3 * part, main)] = tn(attended_grad[...], value_mix[:, side]).astype(half)
    leaving += store_terms(spot, terms, term_outs, 3 * part, main, store_sems, 48)
    wait_all(leaving)


def chain(spot, gathered, mine, theirs, latents, cotangents, vectors, feats, groups):
    blocks, layout = gathered
    rows, width = mine.shape[0], vectors.shape[1]
    part = width // 2
    lanes = 3 * part + main
    outs = term_shapes(groups, width // groups, lanes)
    bits = pltpu.VMEM((rows, width), half)
    result = pl.pallas_call(
        functools.partial(chain_kernel, len(blocks), layout, len(outs), feats),
        out_shape=[
            shape((rows // 2, width), single),
            shape((rows // 2, width), single),
            shape((rows, main + rest), half),
            shape((rows, 128), single),
            shape((8, width), single),
        ]
        + outs,
        in_specs=[scalars] + [remote] * (len(blocks) + 6) + [whole],
        out_specs=[remote] * 2 + [whole] * 3 + [remote] * len(outs),
        scratch_shapes=[
            pltpu.VMEM((2, width, part + main), half),
            pltpu.VMEM((2, width, 2 * part), half),
            pltpu.VMEM((2, rows // 2, width), single),
            pltpu.VMEM((2, rows // 2, width), single),
            pltpu.VMEM((2, rows, main + rest), single),
        ]
        + [bits] * 7
        + [pltpu.VMEM((rows, 2 * main), half)]
        + [pltpu.VMEM((2, rows // 2, width), single)]
        + [pltpu.VMEM((rows // 2, width), single)] * 2
        + [pltpu.VMEM((2, rows // 2, width), single)]
        + [pltpu.VMEM((width, lanes), half)]
        + [pltpu.SemaphoreType.DMA((64,)), pltpu.SemaphoreType.DMA((64,)), pltpu.SemaphoreType.DMA((6,))],
        compiler_params=params,
        cost_estimate=cost(17),
        name="chain",
    )(spot, *blocks, mine, theirs, *latents, *cotangents, vectors)
    return result[:5], result[5:]


def pixel_back_kernel(scale, turn, turns, *refs):
    (query_pix, grad_pix, stats, values_in, keep, pixels, gain, pixel_stats), refs = refs[:8], refs[8:]
    if turn > 0:
        (score_before, sums_before, _), refs = refs[:3], refs[3:]
    score_pix, sums, pixels_grad, values, held, made, score_grads, query_t, grad_t, slope, shift, sems = refs
    feats, count = held.shape
    over = feats - main
    some = main + 16
    step = 512
    origin = turn * count
    here = pl.ds(origin, count)
    early = copy_all([(values_in.at[:, here], values)], sems)
    late = copy_all([(pixels.at[:, 0, here], held)], sems, 1)
    query_t[...] = jnp.transpose(query_pix[...].astype(single))[:some].astype(half)
    grad_t[...] = jnp.transpose(grad_pix[...].astype(single))[:some].astype(half)
    slope[...] = jnp.zeros_like(slope)
    shift[...] = jnp.zeros_like(shift)
    log_total, inner = stats[:, 0:1], stats[:, 1:2]
    wait_all(early)

    def products(start):
        some_values = values[:, pl.ds(pl.multiple_of(start, step), step)]
        return nn(query_pix[...], some_values), nn(grad_pix[...], some_values)

    def norm_back(start, grad):
        lanes = pl.ds(pl.multiple_of(start, step), step)
        there = pl.ds(pl.multiple_of(origin + start, step), step)
        mean, inverse = pixel_stats[0:1, there], pixel_stats[1:2, there]
        unit_a = (held[pl.ds(0, main), lanes] - mean) * inverse
        unit_b = (held[pl.ds(main, over), lanes] - mean) * inverse
        grad_a, grad_b = grad[:main], grad[main : main + over]
        for rows, g, u in ((pl.ds(0, main), grad_a, unit_a), (pl.ds(main, over), grad_b, unit_b)):
            product = g * u
            slope[rows, :] += sum(product[:, 128 * j : 128 * j + 128] for j in range(step // 128))
            shift[rows, :] += sum(g[:, 128 * j : 128 * j + 128] for j in range(step // 128))
        scaled_a, scaled_b = grad_a * gain[pl.ds(0, main)], grad_b * gain[pl.ds(main, over)]
        flat = (jnp.sum(scaled_a, axis=0, keepdims=True) + jnp.sum(scaled_b, axis=0, keepdims=True)) / feats
        along = (
            jnp.sum(scaled_a * unit_a, axis=0, keepdims=True) + jnp.sum(scaled_b * unit_b, axis=0, keepdims=True)
        ) / feats
        made[pl.ds(0, main), lanes] = inverse * (scaled_a - flat - unit_a * along)
        made[pl.ds(main, over), lanes] = inverse * (scaled_b - flat - unit_b * along)

    def leaving(i):
        lanes = pl.ds(pl.multiple_of(2 * i * step, step), 2 * step)
        there = pl.ds(pl.multiple_of(origin + 2 * i * step, step), 2 * step)
        return pltpu.make_async_copy(made.at[:, lanes], pixels_grad.at[:, 0, there], sems.at[2 + i])

    wait_all(late)

    @pl.loop(0, count // (2 * step))
    def _(i):
        starts = [(2 * i + k) * step for k in range(2)]
        now, grads = products(starts[0]), []
        for k, start in enumerate(starts):
            scores, weight_grad = now
            if k == 0:
                now = products(starts[1])
            lanes = pl.ds(pl.multiple_of(start, step), step)
            kept = keep[:, pl.ds(pl.multiple_of(origin + start, step), step)] > 0
            attn = jnp.exp(jnp.where(kept, scores, masked_score) - log_total)
            score_grad = (attn * (weight_grad - inner)).astype(half)
            score_grads[:, lanes] = score_grad
            grads.append(nn(query_t[...], score_grad) + nn(grad_t[...], attn.astype(half)))
        for start, grad in zip(starts, grads):
            norm_back(start, grad)
        leaving(i).start()

    value = nt(score_grads[...], values[...])
    if turn > 0:
        value = value + score_before[...]
    score_pix[...] = value * scale if turn == turns - 1 else value
    lane = lax.broadcasted_iota(jnp.int32, (feats, 128), 1)
    both = jnp.where(
        lane == 0,
        jnp.sum(slope[...], axis=-1, keepdims=True),
        jnp.sum(shift[...], axis=-1, keepdims=True),
    )
    sums[...] = both + sums_before[...] if turn > 0 else both

    @pl.loop(0, count // (2 * step))
    def _(i):
        leaving(i).wait()


def pixel_back(query_pix, grad_pix, stats, normed, keep, pixels, gain, pixel_stats, scale, turn, turns, before):
    feats, _, count = pixels.shape
    rows = query_pix.shape[0]
    held = pltpu.VMEM((feats, count // turns), single)
    return pl.pallas_call(
        functools.partial(pixel_back_kernel, scale, turn, turns),
        out_shape=[shape((rows, main + rest), single), shape((feats, 128), single), shape(pixels.shape, single)],
        in_specs=[whole] * 3 + [remote, whole, remote, whole, whole] + [whole, whole, remote][: len(before)],
        out_specs=[whole, whole, remote],
        scratch_shapes=[
            pltpu.VMEM((main + rest, count // turns), half),
            held,
            held,
            pltpu.VMEM((rows, count // turns), half),
            pltpu.VMEM((main + 16, rows), half),
            pltpu.VMEM((main + 16, rows), half),
            pltpu.VMEM((feats, 128), single),
            pltpu.VMEM((feats, 128), single),
            pltpu.SemaphoreType.DMA((2 + count // turns // 512,)),
        ],
        input_output_aliases={10: 2} if before else {},
        compiler_params=params_most,
        cost_estimate=cost(18 / turns),
        name="pixel_back",
    )(query_pix, grad_pix, stats, normed, keep, pixels, gain, pixel_stats, *before)


def query_back_kernel(count, layout, terms_count, spot, *refs):
    blocks, refs = refs[:count], refs[count:]
    mine, theirs, query_in, normed_mine, normed_theirs, latents_in, grad_in, vectors, *refs = refs
    latents_grad, sums, *refs = refs
    term_outs, refs = refs[:terms_count], refs[terms_count:]
    weights, score_pix, query, normed, latents, middle_grad, query_grad, wide, terms, sems, store_sems, more = refs
    ready = load_blocks(spot, blocks, layout, weights, 0, sems)
    rows_all, width = query.shape
    step = rows_all // 2
    part = width // 2
    score_pix[:, pl.ds(main + rest, rest)] = jnp.zeros((rows_all, rest), half)
    for t in range(2):
        rows, other = pl.ds(t * step, step), pl.ds((1 - t) * step, step)
        score_pix[rows, pl.ds(0, main + rest)] = (mine[rows, :] + theirs[other, :]).astype(half)
    wait_all(ready)
    later = copy_all([(normed_mine, normed.at[0]), (normed_theirs, normed.at[1]), (query_in, query)], more)
    last = copy_all([(latents_in, latents), (grad_in, middle_grad)], more, 3)
    value = nt(score_pix[:, pl.ds(0, main)], weights[0, :, pl.ds(part, main)])
    value = value + nt(score_pix[:, pl.ds(main, rest)], weights[1, :, pl.ds(part, rest)])
    query_grad[...] = value.astype(half)
    wait_all(later)
    side = pl.ds(pl.multiple_of(spot[1] * part, part), part)
    value = tn(query_grad[pl.ds(0, step), :], normed[0, :, side])
    terms[:, pl.ds(0, part)] = (value + tn(query_grad[pl.ds(step, step), :], normed[1, :, side])).astype(half)
    leaving = store_terms(spot, terms, term_outs, 0, part, store_sems, 0)
    side = pl.ds(pl.multiple_of(spot[1] * main, main), main)
    terms[:, pl.ds(part, main)] = tn(query[...], score_pix[:, side]).astype(half)
    leaving += store_terms(spot, terms, term_outs, part, main, store_sems, 16)
    value = query_grad[pl.ds(0, step), :]
    wide[:, pl.ds(0, part)] = nn(value, weights[0, :, pl.ds(0, part)])
    wide[:, pl.ds(part, part)] = nn(value, weights[1, :, pl.ds(0, part)])
    wait_all(last)
    unit, inverse = standard(latents[...])
    grad = wide[...]
    latents_grad[...] = middle_grad[...] + standard_back(grad, vectors[0:1, :], unit, inverse)
    sums[...] = jnp.zeros_like(sums)
    sums[0:1, :] = jnp.sum(grad * unit, axis=0, keepdims=True)
    sums[1:2, :] = jnp.sum(grad, axis=0, keepdims=True)
    wait_all(leaving)


def query_back(spot, gathered, mine, theirs, query, normed, latents, middle_grad, vectors, groups):
    blocks, layout = gathered
    rows, width = query.shape
    lanes = width // 2 + main
    outs = term_shapes(groups, width // groups, lanes)
    one = pltpu.VMEM((rows // 2, width), single)
    result = pl.pallas_call(
        functools.partial(query_back_kernel, len(blocks), layout, len(outs)),
        out_shape=[shape((rows // 2, width), single), shape((8, width), single)] + outs,
        in_specs=[scalars] + [remote] * len(blocks) + [whole] * 2 + [remote] * 5 + [whole],
        out_specs=[whole] * 2 + [remote] * len(outs),
        scratch_shapes=[
            pltpu.VMEM((2, width, lanes), half),
            pltpu.VMEM((rows, 2 * main), half),
            pltpu.VMEM((rows, width), half),
            pltpu.VMEM((2, rows // 2, width), half),
            one,
            one,
            pltpu.VMEM((rows, width), half),
            one,
            pltpu.VMEM((width, lanes), half),
            pltpu.SemaphoreType.DMA((32,)),
            pltpu.SemaphoreType.DMA((32,)),
            pltpu.SemaphoreType.DMA((5,)),
        ],
        compiler_params=params_all,
        cost_estimate=cost(7),
        name="query_back",
    )(spot, *blocks, mine, theirs, query, *normed, latents, middle_grad, vectors)
    return result[:2], result[2:]


def moments_kernel(feats, *refs):
    spot, late_mine, late_theirs, early_mine, early_theirs, vectors, *refs = refs
    square_p, square_m, square_v, pixel_p, pixel_m, pixel_v, *refs = refs
    square_outs, pixel_outs, sums = refs[:4], refs[4:8], refs[8]
    width = square_p.shape[2]
    part = width // 2
    first = spot[1] == 0
    lane = lax.broadcasted_iota(jnp.int32, (1, width), 1)
    row = jnp.zeros((1, width), single)
    for m in range(6):
        mine, theirs = (late_mine, late_theirs) if m in (0, 4) else (early_mine, early_theirs)
        if m < 4:
            lanes = pl.ds(max(m - 1, 0) * part, part)
            sides, outs, k = (pl.ds(0, part), pl.ds(part, part)), square_outs, m
            params_now, first_now, second_now = square_p, square_m, square_v
        else:
            lanes = pl.ds(part if m == 4 else 3 * part, main)
            sides, outs, k = (pl.ds(0, main), pl.ds(main, feats - main)), pixel_outs, m - 4
            params_now, first_now, second_now = pixel_p, pixel_m, pixel_v
        own, other = mine[:, lanes], theirs[:, lanes]
        weight_total, update_total = jnp.zeros((1, 1), single), jnp.zeros((1, 1), single)
        for side, grad in zip(sides, (jnp.where(first, own, other), jnp.where(first, other, own))):
            grad = grad[:, : side.size]
            weight = params_now[k, :, side]
            first_new, second_new, ratio = adam_moments(grad, first_now[k, :, side], second_now[k, :, side])
            update = ratio + decay_rate * weight
            for out, value in zip(outs, (grad, first_new, second_new, update)):
                out[k, :, side] = value
            weight_total = weight_total + jnp.sum(weight * weight, keepdims=True)
            update_total = update_total + jnp.sum(update * update, keepdims=True)
        row = row + jnp.where(lane == part + m, weight_total, jnp.where(lane == part + 6 + m, update_total, 0.0))
    sums[...] = vectors[...]
    sums[7:8, pl.ds(part, part)] = row[:, part:]


def moments(spot, late, early, vectors, square, pixel):
    big, small = shape(square[0].shape, single), shape(pixel[0].shape, single)
    return pl.pallas_call(
        functools.partial(moments_kernel, pixel[0].shape[2]),
        out_shape=[big] * 4 + [small] * 4 + [shape((8, big.shape[2]), single)],
        in_specs=[scalars] + [whole] * 11,
        out_specs=[whole] * 9,
        compiler_params=params,
        cost_estimate=cost(5),
        name="moments",
    )(spot, *late, *early, vectors, *square, *pixel)


def apply_kernel(sums, square_p, square_u, pixel_p, pixel_u, *refs):
    states, outs = refs[:6], refs[6:]
    square_new, square_copy, pixel_new, pixel_copy, norms, *news = outs
    part = sums.shape[1] // 2
    squares = sums[7:8, pl.ds(part, 128)]
    weight_norm, update_norm = jnp.sqrt(squares[:, 0:6]), jnp.sqrt(squares[:, 6:12])
    trust = weight_norm / (update_norm + epsilon)
    for row, value in enumerate((weight_norm, update_norm, trust)):
        norms[row : row + 1, :] = value
    for m in range(6):
        k, weight, update, new, copy = (
            (m, square_p, square_u, square_new, square_copy)
            if m < 4
            else (m - 4, pixel_p, pixel_u, pixel_new, pixel_copy)
        )
        value = weight[k] - learn_rate * trust[:, m : m + 1] * update[k]
        new[k] = value
        copy[k] = value.astype(half)
    feats = states[3].shape[1]
    for grad, (value, first, second), out in (
        (sums[0:6, :], states[:3], news[:3]),
        (sums[6:8, 0:feats], states[3:], news[3:]),
    ):
        first_new, second_new, ratio = adam_moments(grad, first[...], second[...])
        out[0][...] = value[...] - vector_rate * ratio
        out[1][...] = first_new
        out[2][...] = second_new


def apply(sums, square_p, square_u, pixel_p, pixel_u, vectors, norms):
    outs = [(square_p, single), (square_p, half), (pixel_p, single), (pixel_p, half)]
    states = [*vectors, *norms]
    return pl.pallas_call(
        apply_kernel,
        out_shape=[shape(a.shape, dtype) for a, dtype in outs]
        + [shape((3, 6), single)]
        + [shape(a.shape, single) for a in states],
        in_specs=[whole] * 11,
        out_specs=[whole] * 11,
        compiler_params=params,
        cost_estimate=cost(4),
        name="apply",
    )(sums, square_p, square_u, pixel_p, pixel_u, *states)


def local(
    latents,
    pixels,
    keep_mask,
    cotangent,
    square_weights,
    square_first,
    square_second,
    pixel_weights,
    pixel_first,
    pixel_second,
    latent_vectors,
    latent_first,
    latent_second,
    pixel_norm,
    pixel_norm_first,
    pixel_norm_second,
):
    width = latents.shape[2]
    feats = pixels.shape[2]
    scale = width ** (-0.5)
    rank = lax.axis_index("seq")
    groups = lax.axis_size("dp")
    spot = jnp.stack([lax.axis_index("dp"), rank]).astype(jnp.int32)

    def turned(array):
        return jnp.transpose(array, (0, 2, 1))

    square = [turned(array) for array in (square_weights, square_first, square_second)]
    pixel = [turned(array) for array in (pixel_weights, pixel_first, pixel_second)]

    latents_two = (latents[0], trade(latents[0]))
    cotangent_two = (cotangent[0], trade(cotangent[0]))
    pixels_t = jnp.transpose(pixels, (2, 0, 1))
    gain, shift = pixel_norm[0][:, None], pixel_norm[1][:, None]
    pixel_normed, pixel_stats = norm_pixels(pixels_t, gain, shift)
    normed = norm_latents(latents[0], latent_vectors)
    normed = (normed, trade(normed))
    blocks = gather_matrices(pack(spot, square[0], pixel[0]), pixel_normed, normed[0])
    query, query_pix, sent = attend(spot, blocks, normed, pixel_normed, keep_mask, scale, feats)
    (latents_out, middle_grad, grad_pix, stats, chain_sums), early_terms = chain(
        spot, blocks, sent, trade(sent), latents_two, cotangent_two, latent_vectors, feats, groups
    )
    pixel_args = (query_pix, grad_pix, stats, pixel_normed, keep_mask, pixels_t, gain, pixel_stats, scale)
    turn_one = pixel_back(*pixel_args, 0, 2, ())
    if len(early_terms) > 1:
        *early_got, score_pix = tie([*send_first(early_terms), turn_one[0]], turn_one[1])
        turn_two = pixel_back(*pixel_args, 1, 2, [score_pix, *turn_one[1:]])
        early_got = send_second(early_terms, early_got, turn_two[0])
    else:
        turn_two, early_got = pixel_back(*pixel_args, 1, 2, turn_one), None
    score_pix, pixel_sums, pixels_grad = turn_two
    (latents_grad, query_sums), late_terms = query_back(
        spot, blocks, score_pix, trade(score_pix), query, normed, latents[0], middle_grad, latent_vectors, groups
    )
    early_got = send_third(early_terms, early_got)
    if len(late_terms) > 1:
        tied = tie([*late_terms[:3], *early_got], late_terms[3])
        late_terms, early_got = [*tied[:3], *late_terms[3:]], tied[3:]
    early = sum_own(early_terms, early_got)
    late = sum_own(late_terms, send_third(late_terms, send_second(late_terms, send_first(late_terms))))

    norm_terms = jnp.pad(jnp.transpose(pixel_sums[:, :2]), ((6, 0), (0, width - feats)))
    vector_terms = chain_sums + query_sums + norm_terms
    vector_terms = vector_terms + trade(vector_terms)
    square_grad, square_first_new, square_second_new, square_u, *rest_outs = moments(
        spot, (late, trade(late)), (early, trade(early)), vector_terms, square, pixel
    )
    pixel_weight_grad, pixel_first_new, pixel_second_new, pixel_u, sums = rest_outs
    square_new, square_copy, pixel_new, pixel_copy, matrix_norms, *news = apply(
        sum_all(sums),
        square[0],
        square_u,
        pixel[0],
        pixel_u,
        (latent_vectors, latent_first, latent_second),
        (pixel_norm, pixel_norm_first, pixel_norm_second),
    )
    latent_vectors_new, latent_first_new, latent_second_new = news[:3]
    pixel_norm_new, pixel_norm_first_new, pixel_norm_second_new = news[3:]
    return (
        latents_out[None],
        latents_grad[None],
        jnp.transpose(pixels_grad, (1, 2, 0)),
        turned(square_grad),
        turned(square_first_new),
        turned(square_second_new),
        turned(square_new),
        turned(square_copy),
        turned(pixel_weight_grad),
        turned(pixel_first_new),
        turned(pixel_second_new),
        turned(pixel_new),
        turned(pixel_copy),
        latent_first_new,
        latent_second_new,
        latent_vectors_new,
        pixel_norm_first_new,
        pixel_norm_second_new,
        pixel_norm_new,
        matrix_norms,
    )


def solution(mesh):
    return jax.shard_map(
        local,
        mesh=mesh,
        in_specs=(
            P("dp", "seq", None),
            P("dp", "seq", None),
            P("dp", "seq"),
            P("dp", "seq", None),
            P(None, None, "dp"),
            P(None, None, "dp"),
            P(None, None, "dp"),
            P(None, None, "dp"),
            P(None, None, "dp"),
            P(None, None, "dp"),
            P(),
            P(),
            P(),
            P(),
            P(),
            P(),
        ),
        out_specs=(
            P("dp", "seq", None),
            P("dp", "seq", None),
            P("dp", "seq", None),
            P(None, None, "dp"),
            P(None, None, "dp"),
            P(None, None, "dp"),
            P(None, None, "dp"),
            P(None, None, "dp"),
            P(None, None, "dp"),
            P(None, None, "dp"),
            P(None, None, "dp"),
            P(None, None, "dp"),
            P(None, None, "dp"),
            P(),
            P(),
            P(),
            P(),
            P(),
            P(),
            P(),
        ),
        check_vma=False,
    )
```

profile of v0, /device:TPU:0, one launch (start us, length us, event | category | flops | bytes accessed | tf_op | source)
XLA Modules:
  0.0 194.6 jit_solution(16313295464916928902)
XLA Ops:
  0.8 1.2 copy-done.8
  3.5 3.0 %collective-permute-start.4 = (bf16[64,2560]{1,0:T(8,128)(2,1)S(1)}, bf16[64,2560]{1,0:T(8,128)(2,1)S(1)}, u32[]{:S(2)}, u32[]{:S(2)}) collective-permute-start(bf16[64,2560]{1,0:T(8,128)(2,1)S(1)} %pack.1.refs_0_), channel_id=1, source_target_pairs={{0,2},{2,0},{4,6},{6,4},{8,10},{10,8},{12,14},{14,12},{16,18},{18,... | collective-permute-start | bytes 983048 | tf_op jit(solution)/shard_map/ppermute | solution.py:71
  6.5 1.5 collective-permute-start.3
  8.0 2.0 %collective-permute-start.1 = (bf16[64,2560]{1,0:T(8,128)(2,1)S(1)}, bf16[64,2560]{1,0:T(8,128)(2,1)S(1)}, u32[]{:S(2)}, u32[]{:S(2)}) collective-permute-start(bf16[64,2560]{1,0:T(8,128)(2,1)S(1)} %pack.1.refs_0_), channel_id=1, source_target_pairs={{0,8},{2,10},{4,12},{6,14},{8,0},{10,2},{12,4},{14,6},{16,24},{18,... | collective-permute-start | bytes 983048 | tf_op jit(solution)/shard_map/ppermute | solution.py:71
  10.1 2.6 %collective-permute-start = (bf16[64,2560]{1,0:T(8,128)(2,1)S(1)}, bf16[64,2560]{1,0:T(8,128)(2,1)S(1)}, u32[]{:S(2)}, u32[]{:S(2)}) collective-permute-start(bf16[64,2560]{1,0:T(8,128)(2,1)S(1)} %pack.1.refs_0_), channel_id=1, source_target_pairs={{0,16},{2,18},{4,20},{6,22},{8,24},{10,26},{12,28},{14,30},{16,0},... | collective-permute-start | bytes 983048 | tf_op jit(solution)/shard_map/ppermute | solution.py:71
  13.0 2.3 %copy-done.2 = f32[1,4096,261]{1,0,2:T(1,128)S(1)} copy-done((f32[1,4096,261]{1,0,2:T(1,128)S(1)}, f32[1,4096,261]{1,0,2:T(1,128)}, u32[]{:S(2)}) %copy-start.2) | copy-done | bytes 4276248
  15.2 5.6 %norm_pixels.1 = (bf16[384,4096]{1,0:T(8,128)(2,1)S(1)}, f32[2,4096]{1,0:T(2,128)S(1)}) custom-call(f32[261,1,4096]{2,1,0:T(1,128)S(1)} %bitcast.32, f32[261,1]{1,0:T(8,128)S(1)} %copy.53.gain.refs_6_, f32[261,1]{1,0:T(8,128)S(1)} %copy.54.shift), custom_call_target="tpu_custom_call" | custom-call | flops 7699999744 | bytes 1024 | tf_op jit(solution)/shard_map/norm_pixels/pallas_call | solution.py:356
  20.9 1.6 collective-permute-done.2.refs_3_.refs_0_
  22.5 1.3 collective-permute-done.1.refs_2_.refs_1_
  23.8 2.6 %collective-permute-done.refs_1_.refs_2_ = bf16[64,2560]{1,0:T(8,128)(2,1)S(1)} collective-permute-done((bf16[64,2560]{1,0:T(8,128)(2,1)S(1)}, bf16[64,2560]{1,0:T(8,128)(2,1)S(1)}, u32[]{:S(2)}, u32[]{:S(2)}) %collective-permute-start) | collective-permute-done | bytes 327712 | tf_op jit(solution)/shard_map/ppermute | solution.py:71
  27.2 1.5 collective-permute-start.10
  28.7 1.5 collective-permute-start.8
  32.4 7.6 %collective-permute-done.6.refs_0_.refs_2_ = bf16[128,2560]{1,0:T(8,128)(2,1)S(1)} collective-permute-done((bf16[128,2560]{1,0:T(8,128)(2,1)S(1)}, bf16[128,2560]{1,0:T(8,128)(2,1)S(1)}, u32[]{:S(2)}, u32[]{:S(2)}) %collective-permute-start.6) | collective-permute-done | bytes 655392 | tf_op jit(solution)/shard_map/ppermute | solution.py:71
  40.0 1.3 collective-permute-done.10.refs_2_.refs_6_
  41.4 1.7 collective-permute-done.8.refs_1_.refs_4_
  44.4 1.5 collective-permute-start.14
  45.9 10.3 %collective-permute-done.12.refs_8_ = bf16[64,2560]{1,0:T(8,128)(2,1)S(1)} collective-permute-done((bf16[64,2560]{1,0:T(8,128)(2,1)S(1)}, bf16[64,2560]{1,0:T(8,128)(2,1)S(1)}, u32[]{:S(2)}, u32[]{:S(2)}) %collective-permute-start.12) | collective-permute-done | bytes 327712 | tf_op jit(solution)/shard_map/ppermute | solution.py:71
  59.4 1.3 collective-permute-done.13.refs_9_
  61.2 9.1 %attend.1 = (bf16[512,1024]{1,0:T(8,128)(2,1)S(1)}, bf16[512,384]{1,0:T(8,128)(2,1)S(1)}, f32[512,384]{1,0:T(8,128)S(1)}) custom-call(s32[2]{0:T(128)S(1)} %pad_add_fusion.1.spot.refs_0_, bf16[384,2560]{1,0:T(8,128)(2,1)S(1)} %stack.15.refs_0_, bf16[384,2560]{1,0:T(8,128)(2,1)S(1)} %collective-permute-done.5.refs_1_, ...), custom_call_target="tpu_custom_call" | custom-call | flops 12099999744 | bytes 1024 | tf_op jit(solution)/shard_map/attend/pallas_call | solution.py:438
  72.2 2.1 %collective-permute-done.19.refs_15_ = f32[512,384]{1,0:T(8,128)S(1)} collective-permute-done((f32[512,384]{1,0:T(8,128)S(1)}, f32[512,384]{1,0:T(8,128)S(1)}, u32[]{:S(2)}, u32[]{:S(2)}) %collective-permute-start.19) | collective-permute-done | bytes 786464 | tf_op jit(solution)/shard_map/ppermute | solution.py:75
  74.4 18.2 %chain.1 = (f32[256,1024]{1,0:T(8,128)}, f32[256,1024]{1,0:T(8,128)S(1)}, bf16[512,384]{1,0:T(8,128)(2,1)S(1)}, f32[512,128]{1,0:T(8,128)S(1)}, f32[8,1024]{1,0:...) custom-call(s32[2]{0:T(128)S(1)} %pad_add_fusion.1.spot.refs_0_, ...), custom_call_target="tpu_custom_call" | custom-call | flops 18699999232 | bytes 1024 | tf_op jit(solution)/shard_map/chain/pallas_call | solution.py:586
  95.1 1.5 collective-permute-start.23
  97.6 1.3 collective-permute-start.31
  98.9 10.5 %pixel_back.2 = (f32[512,384]{1,0:T(8,128)}, f32[261,128]{1,0:T(8,128)}, f32[261,1,4096]{2,1,0:T(1,128)}) custom-call(bf16[512,384]{1,0:T(8,128)(2,1)} %copy-done.42, bf16[512,384]{1,0:T(8,128)(2,1)} %copy-done.43, f32[512,128]{1,0:T(8,128)} %copy-done.44, bf16[384,4096]{1,0:T(8,128)(2,1)} %copy-done.39, s32[1,4096]{1,0:T(1,128)} %refs_4_.4, ...), custom_call_target="tpu_custom_call" | custom-call | flops 9900000256 | bytes 1024 | tf_op jit(solution)/shard_map/pixel_back/pallas_call | solution.py:708
  115.1 10.8 %pixel_back.3 = (f32[512,384]{1,0:T(8,128)}, f32[261,128]{1,0:T(8,128)}, f32[261,1,4096]{2,1,0:T(1,128)}) custom-call(bf16[512,384]{1,0:T(8,128)(2,1)} %copy-done.42, bf16[512,384]{1,0:T(8,128)(2,1)} %copy-done.43, f32[512,128]{1,0:T(8,128)} %copy-done.44, bf16[384,4096]{1,0:T(8,128)(2,1)} %copy-done.39, ...), custom_call_target="tpu_custom_call", output_to_operand_aliasing={{2}: (10, {})} | custom-call | flops 9900000256 | bytes 1024 | tf_op jit(solution)/shard_map/pixel_back/pallas_call | solution.py:708
  126.0 1.5 collective-permute-start.29
  127.5 1.5 collective-permute-start.30
  130.6 2.5 %add_convert_fusion.2 = (bf16[64,1792]{1,0:T(8,128)(2,1)}, bf16[64,1792]{1,0:T(8,128)(2,1)}, bf16[64,1792]{1,0:T(8,128)(2,1)}) fusion(bf16[64,1792]{1,0:T(8,128)(2,1)S(1)} %get-tuple-element.148, bf16[128,1792]{1,0:T(8,128)(2,1)} %get-tuple-element.147, bf16[128,1792]{1,0:T(8,128)(2,1)} %get-tuple-element.145, bf16[128,1792]{1,0:T(8,128)(2,1)} %get-tuple-element.144, ...), kind=kLoop, calls=%fused_computation.3 | loop fusion | flops 2064384 | bytes 2752512 | tf_op jit(solution)/shard_map/convert_element_type | solution.py:289
  133.0 1.2 collective-permute-start.36
  134.3 2.0 %collective-permute-start.34 = (bf16[64,1792]{1,0:T(8,128)(2,1)}, bf16[64,1792]{1,0:T(8,128)(2,1)}, u32[]{:S(2)}, u32[]{:S(2)}) collective-permute-start(bf16[64,1792]{1,0:T(8,128)(2,1)} %get-tuple-element.185), channel_id=1, source_target_pairs={{0,8},{2,10},{4,12},{6,14},{8,0},{10,2},{12,4},{14,6},{16,24},{18,... | collective-permute-start | bytes 688136 | tf_op jit(solution)/shard_map/ppermute | solution.py:71
  137.3 8.9 %query_back.1 = (f32[256,1024]{1,0:T(8,128)}, f32[8,1024]{1,0:T(8,128)}, bf16[128,768]{1,0:T(8,128)(2,1)}, bf16[64,768]{1,0:T(8,128)(2,1)}, bf16[64,768]{1,0:T(8...) custom-call(s32[2]{0:T(128)} %copy-done.37, ...), custom_call_target="tpu_custom_call" | custom-call | flops 7699999744 | bytes 1024 | tf_op jit(solution)/shard_map/query_back/pallas_call | solution.py:778
  148.4 1.5 collective-permute-start.28
  151.3 3.5 %collective-permute-done.37 = bf16[128,768]{1,0:T(8,128)(2,1)} collective-permute-done((bf16[128,768]{1,0:T(8,128)(2,1)}, bf16[128,768]{1,0:T(8,128)(2,1)}, u32[]{:S(2)}, u32[]{:S(2)}) %collective-permute-start.37) | collective-permute-done | bytes 196640 | tf_op jit(solution)/shard_map/ppermute | solution.py:71
  156.8 1.3 collective-permute-start.38
  161.3 2.3 %collective-permute-done.38 = bf16[128,768]{1,0:T(8,128)(2,1)S(1)} collective-permute-done((bf16[128,768]{1,0:T(8,128)(2,1)S(1)}, bf16[128,768]{1,0:T(8,128)(2,1)S(1)}, u32[]{:S(2)}, u32[]{:S(2)}) %collective-permute-start.38) | collective-permute-done | bytes 196640 | tf_op jit(solution)/shard_map/ppermute | solution.py:71
  163.6 1.3 collective-permute-done.42
  166.0 1.8 collective-permute-start.44
  167.8 2.0 %collective-permute-start.43 = (bf16[64,768]{1,0:T(8,128)(2,1)S(1)}, bf16[64,768]{1,0:T(8,128)(2,1)S(1)}, u32[]{:S(2)}, u32[]{:S(2)}) collective-permute-start(bf16[64,768]{1,0:T(8,128)(2,1)S(1)} %get-tuple-element.191), channel_id=1, source_target_pairs={{0,6},{2,4},{4,2},{6,0},{8,14},{10,12},{12,10},{14,8},{16,22},{18,... | collective-permute-start | bytes 294920 | tf_op jit(solution)/shard_map/ppermute | solution.py:71
  169.8 1.5 convert_add_fusion.refs_3_
  171.7 1.6 collective-permute-done.43
  175.1 4.1 %moments.1 = (f32[4,64,1024]{2,1,0:T(8,128)}, f32[4,64,1024]{2,1,0:T(8,128)}, f32[4,64,1024]{2,1,0:T(8,128)}, f32[4,64,1024]{2,1,0:T(8,128)S(1)}, f32[2,64,261]{...) custom-call(s32[2]{0:T(128)S(1)} %copy-done.38, ...), custom_call_target="tpu_custom_call" | custom-call | flops 5500000256 | bytes 1024 | tf_op jit(solution)/shard_map/moments/pallas_call | solution.py:841
  179.2 2.0 %collective-permute-start.50 = (f32[8,1024]{1,0:T(8,128)S(1)}, f32[8,1024]{1,0:T(8,128)S(1)}, u32[]{:S(2)}, u32[]{:S(2)}) collective-permute-start(f32[8,1024]{1,0:T(8,128)S(1)} %get-tuple-element.167), channel_id=1, source_target_pairs={{0,6},{2,4},{4,2},{6,0},{8,14},{10,12},{12,10},{14,8},{16,22},{18,... | collective-permute-start | bytes 98312 | tf_op jit(solution)/shard_map/ppermute | solution.py:71
  182.7 1.3 collective-permute-done.50
  185.7 2.5 %collective-permute-start.53 = (f32[8,1024]{1,0:T(8,128)S(1)}, f32[8,1024]{1,0:T(8,128)S(1)}, u32[]{:S(2)}, u32[]{:S(2)}) collective-permute-start(f32[8,1024]{1,0:T(8,128)S(1)} %add_add_fusion.1), channel_id=1, source_target_pairs={{0,24},{2,26},{4,28},{6,30},{8,16},{10,18},{12,20},{14,22},{16,8},... | collective-permute-start | bytes 98312 | tf_op jit(solution)/shard_map/ppermute | solution.py:71
  188.2 1.9 collective-permute-start.51
  190.1 1.3 collective-permute-done.53
  191.4 1.6 collective-permute-done.52
  193.1 1.6 apply.1
  (210 shorter events, 38.1 us)
Async XLA Ops:
  3.5 26.7 %collective-permute-start.4 = (bf16[64,2560]{1,0:T(8,128)(2,1)S(1)}, bf16[64,2560]{1,0:T(8,128)(2,1)S(1)}, u32[]{:S(2)}, u32[]{:S(2)}) collective-permute-start(bf16[64,2560]{1,0:T(8,128)(2,1)S(1)} %pack.1.refs_0_), channel_id=1, source_target_pairs={{0,2},{2,0},{4,6},{6,4},{8,10},{10,8},{12,14},{14,12},{16,18},{18,... | collective-permute-start | bytes 983048 | tf_op jit(solution)/shard_map/ppermute | solution.py:71
  6.5 23.7 %collective-permute-start.3 = (bf16[64,2560]{1,0:T(8,128)(2,1)S(1)}, bf16[64,2560]{1,0:T(8,128)(2,1)S(1)}, u32[]{:S(2)}, u32[]{:S(2)}) collective-permute-start(bf16[64,2560]{1,0:T(8,128)(2,1)S(1)} %pack.1.refs_0_), channel_id=1, source_target_pairs={{0,4},{2,6},{4,0},{6,2},{8,12},{10,14},{12,8},{14,10},{16,20},{18,... | collective-permute-start | bytes 983048 | tf_op jit(solution)/shard_map/ppermute | solution.py:71
  8.0 14.5 %collective-permute-start.2 = (bf16[64,2560]{1,0:T(8,128)(2,1)S(1)}, bf16[64,2560]{1,0:T(8,128)(2,1)S(1)}, u32[]{:S(2)}, u32[]{:S(2)}) collective-permute-start(bf16[64,2560]{1,0:T(8,128)(2,1)S(1)} %pack.1.refs_0_), channel_id=1, source_target_pairs={{0,6},{2,4},{4,2},{6,0},{8,14},{10,12},{12,10},{14,8},{16,22},{18,... | collective-permute-start | bytes 983048 | tf_op jit(solution)/shard_map/ppermute | solution.py:71
  8.0 15.8 %collective-permute-start.1 = (bf16[64,2560]{1,0:T(8,128)(2,1)S(1)}, bf16[64,2560]{1,0:T(8,128)(2,1)S(1)}, u32[]{:S(2)}, u32[]{:S(2)}) collective-permute-start(bf16[64,2560]{1,0:T(8,128)(2,1)S(1)} %pack.1.refs_0_), channel_id=1, source_target_pairs={{0,8},{2,10},{4,12},{6,14},{8,0},{10,2},{12,4},{14,6},{16,24},{18,... | collective-permute-start | bytes 983048 | tf_op jit(solution)/shard_map/ppermute | solution.py:71
  10.1 16.4 %collective-permute-start = (bf16[64,2560]{1,0:T(8,128)(2,1)S(1)}, bf16[64,2560]{1,0:T(8,128)(2,1)S(1)}, u32[]{:S(2)}, u32[]{:S(2)}) collective-permute-start(bf16[64,2560]{1,0:T(8,128)(2,1)S(1)} %pack.1.refs_0_), channel_id=1, source_target_pairs={{0,16},{2,18},{4,20},{6,22},{8,24},{10,26},{12,28},{14,30},{16,0},... | collective-permute-start | bytes 983048 | tf_op jit(solution)/shard_map/ppermute | solution.py:71
  26.6 13.4 %collective-permute-start.6 = (bf16[128,2560]{1,0:T(8,128)(2,1)S(1)}, bf16[128,2560]{1,0:T(8,128)(2,1)S(1)}, u32[]{:S(2)}, u32[]{:S(2)}) collective-permute-start(bf16[128,2560]{1,0:T(8,128)(2,1)S(1)} %get-tuple-element.103), channel_id=1, source_target_pairs={{0,8},{2,10},{4,12},{6,14},{8,0},{10,2},{12,4},{14,6},{16,24},{18,... | collective-permute-start | bytes 1966088 | tf_op jit(solution)/shard_map/ppermute | solution.py:71
  27.2 14.2 %collective-permute-start.10 = (bf16[128,2560]{1,0:T(8,128)(2,1)S(1)}, bf16[128,2560]{1,0:T(8,128)(2,1)S(1)}, u32[]{:S(2)}, u32[]{:S(2)}) collective-permute-start(bf16[128,2560]{1,0:T(8,128)(2,1)S(1)} %get-tuple-element.104), channel_id=1, source_target_pairs={{0,2},{2,0},{4,6},{6,4},{8,10},{10,8},{12,14},{14,12},{16,18},{18,... | collective-permute-start | bytes 1966088 | tf_op jit(solution)/shard_map/ppermute | solution.py:71
  28.7 14.4 %collective-permute-start.8 = (bf16[128,2560]{1,0:T(8,128)(2,1)S(1)}, bf16[128,2560]{1,0:T(8,128)(2,1)S(1)}, u32[]{:S(2)}, u32[]{:S(2)}) collective-permute-start(bf16[128,2560]{1,0:T(8,128)(2,1)S(1)} %get-tuple-element.104), channel_id=1, source_target_pairs={{0,4},{2,6},{4,0},{6,2},{8,12},{10,14},{12,8},{14,10},{16,20},{18,... | collective-permute-start | bytes 1966088 | tf_op jit(solution)/shard_map/ppermute | solution.py:71
  31.4 29.8 %collective-permute-start.5 = (bf16[384,2560]{1,0:T(8,128)(2,1)S(1)}, bf16[384,2560]{1,0:T(8,128)(2,1)S(1)}, u32[]{:S(2)}, u32[]{:S(2)}) collective-permute-start(bf16[384,2560]{1,0:T(8,128)(2,1)S(1)} %stack.15.refs_0_), channel_id=1, source_target_pairs={{0,1},{1,0},{2,3},{3,2},{4,5},{5,4},{6,7},{7,6},{8,9},{9,8},{10,11... | collective-permute-start | bytes 5898248 | tf_op jit(solution)/shard_map/ppermute | solution.py:75
  31.9 14.0 %collective-permute-start.18 = (bf16[256,1024]{1,0:T(8,128)(2,1)S(1)}, bf16[256,1024]{1,0:T(8,128)(2,1)S(1)}, u32[]{:S(2)}, u32[]{:S(2)}) collective-permute-start(bf16[256,1024]{1,0:T(8,128)(2,1)S(1)} %norm_latents.1.refs_3_.refs_14_.refs_17_), channel_id=1, source_target_pairs={{0,1},{1,0},{2,3},{3,2},{4,5},{5,4},{6,7},{7,6},{8,9},{9,8},{10,11... | collective-permute-start | bytes 1572872 | tf_op jit(solution)/shard_map/ppermute | solution.py:75
  43.2 13.1 %collective-permute-start.12 = (bf16[64,2560]{1,0:T(8,128)(2,1)S(1)}, bf16[64,2560]{1,0:T(8,128)(2,1)S(1)}, u32[]{:S(2)}, u32[]{:S(2)}) collective-permute-start(bf16[64,2560]{1,0:T(8,128)(2,1)S(1)} %get-tuple-element.105), channel_id=1, source_target_pairs={{0,16},{2,18},{4,20},{6,22},{8,24},{10,26},{12,28},{14,30},{16,0},... | collective-permute-start | bytes 983048 | tf_op jit(solution)/shard_map/ppermute | solution.py:71
  43.8 12.9 %collective-permute-start.16 = (bf16[128,2560]{1,0:T(8,128)(2,1)S(1)}, bf16[128,2560]{1,0:T(8,128)(2,1)S(1)}, u32[]{:S(2)}, u32[]{:S(2)}) collective-permute-start(bf16[128,2560]{1,0:T(8,128)(2,1)S(1)} %get-tuple-element.107), channel_id=1, source_target_pairs={{0,2},{2,0},{4,6},{6,4},{8,10},{10,8},{12,14},{14,12},{16,18},{18,... | collective-permute-start | bytes 1966088 | tf_op jit(solution)/shard_map/ppermute | solution.py:71
  44.4 11.8 %collective-permute-start.14 = (bf16[64,2560]{1,0:T(8,128)(2,1)S(1)}, bf16[64,2560]{1,0:T(8,128)(2,1)S(1)}, u32[]{:S(2)}, u32[]{:S(2)}) collective-permute-start(bf16[64,2560]{1,0:T(8,128)(2,1)S(1)} %get-tuple-element.106), channel_id=1, source_target_pairs={{0,4},{2,6},{4,0},{6,2},{8,12},{10,14},{12,8},{14,10},{16,20},{18,... | collective-permute-start | bytes 983048 | tf_op jit(solution)/shard_map/ppermute | solution.py:71
  45.9 10.9 %collective-permute-start.7 = (bf16[128,2560]{1,0:T(8,128)(2,1)S(1)}, bf16[128,2560]{1,0:T(8,128)(2,1)S(1)}, u32[]{:S(2)}, u32[]{:S(2)}) collective-permute-start(bf16[128,2560]{1,0:T(8,128)(2,1)S(1)} %collective-permute-done.6.refs_0_.refs_2_), channel_id=1, source_target_pairs={{0,1},{1,0},{2,3},{3,2},{4,5},{5,4},{6,7},{7,6},{8,9},{9,8},{10,11... | collective-permute-start | bytes 1966088 | tf_op jit(solution)/shard_map/ppermute | solution.py:75
  56.7 4.4 %collective-permute-start.17 = (bf16[128,2560]{1,0:T(8,128)(2,1)S(1)}, bf16[128,2560]{1,0:T(8,128)(2,1)S(1)}, u32[]{:S(2)}, u32[]{:S(2)}) collective-permute-start(bf16[128,2560]{1,0:T(8,128)(2,1)S(1)} %collective-permute-done.16.refs_12_), channel_id=1, source_target_pairs={{0,1},{1,0},{2,3},{3,2},{4,5},{5,4},{6,7},{7,6},{8,9},{9,8},{10,11... | collective-permute-start | bytes 1966088 | tf_op jit(solution)/shard_map/ppermute | solution.py:75
  56.8 3.8 %collective-permute-start.13 = (bf16[64,2560]{1,0:T(8,128)(2,1)S(1)}, bf16[64,2560]{1,0:T(8,128)(2,1)S(1)}, u32[]{:S(2)}, u32[]{:S(2)}) collective-permute-start(bf16[64,2560]{1,0:T(8,128)(2,1)S(1)} %collective-permute-done.12.refs_8_), channel_id=1, source_target_pairs={{0,1},{1,0},{2,3},{3,2},{4,5},{5,4},{6,7},{7,6},{8,9},{9,8},{10,11... | collective-permute-start | bytes 983048 | tf_op jit(solution)/shard_map/ppermute | solution.py:75
  59.3 12.9 %collective-permute-start.20 = (f32[256,1024]{1,0:T(8,128)S(1)}, f32[256,1024]{1,0:T(8,128)S(1)}, u32[]{:S(2)}, u32[]{:S(2)}) collective-permute-start(f32[256,1024]{1,0:T(8,128)S(1)} %bitcast.36), channel_id=1, source_target_pairs={{0,1},{1,0},{2,3},{3,2},{4,5},{5,4},{6,7},{7,6},{8,9},{9,8},{10,11... | collective-permute-start | bytes 3145736 | tf_op jit(solution)/shard_map/ppermute | solution.py:75
  60.7 11.5 %collective-permute-start.21 = (f32[256,1024]{1,0:T(8,128)S(1)}, f32[256,1024]{1,0:T(8,128)S(1)}, u32[]{:S(2)}, u32[]{:S(2)}) collective-permute-start(f32[256,1024]{1,0:T(8,128)S(1)} %bitcast.48), channel_id=1, source_target_pairs={{0,1},{1,0},{2,3},{3,2},{4,5},{5,4},{6,7},{7,6},{8,9},{9,8},{10,11... | collective-permute-start | bytes 3145736 | tf_op jit(solution)/shard_map/ppermute | solution.py:75
  95.1 14.3 %collective-permute-start.23 = (bf16[64,1792]{1,0:T(8,128)(2,1)S(1)}, bf16[64,1792]{1,0:T(8,128)(2,1)S(1)}, u32[]{:S(2)}, u32[]{:S(2)}) collective-permute-start(bf16[64,1792]{1,0:T(8,128)(2,1)S(1)} %get-tuple-element.115), channel_id=1, source_target_pairs={{0,4},{2,6},{4,0},{6,2},{8,12},{10,14},{12,8},{14,10},{16,20},{18,... | collective-permute-start | bytes 688136 | tf_op jit(solution)/shard_map/ppermute | solution.py:71
  96.6 12.8 %collective-permute-start.24 = (bf16[64,1792]{1,0:T(8,128)(2,1)S(1)}, bf16[64,1792]{1,0:T(8,128)(2,1)S(1)}, u32[]{:S(2)}, u32[]{:S(2)}) collective-permute-start(bf16[64,1792]{1,0:T(8,128)(2,1)S(1)} %get-tuple-element.116), channel_id=1, source_target_pairs={{0,16},{2,18},{4,20},{6,22},{8,24},{10,26},{12,28},{14,30},{16,0},... | collective-permute-start | bytes 688136 | tf_op jit(solution)/shard_map/ppermute | solution.py:71
  96.9 13.4 %collective-permute-start.22 = (bf16[128,1792]{1,0:T(8,128)(2,1)S(1)}, bf16[128,1792]{1,0:T(8,128)(2,1)S(1)}, u32[]{:S(2)}, u32[]{:S(2)}) collective-permute-start(bf16[128,1792]{1,0:T(8,128)(2,1)S(1)} %get-tuple-element.114), channel_id=1, source_target_pairs={{0,2},{2,0},{4,6},{6,4},{8,10},{10,8},{12,14},{14,12},{16,18},{18,... | collective-permute-start | bytes 1376264 | tf_op jit(solution)/shard_map/ppermute | solution.py:71
  97.6 29.9 %collective-permute-start.31 = (bf16[128,1792]{1,0:T(8,128)(2,1)}, bf16[128,1792]{1,0:T(8,128)(2,1)S(1)}, u32[]{:S(2)}, u32[]{:S(2)}) collective-permute-start(bf16[128,1792]{1,0:T(8,128)(2,1)} %get-tuple-element.138), channel_id=1, source_target_pairs={{0,2},{2,0},{4,6},{6,4},{8,10},{10,8},{12,14},{14,12},{16,18},{18,... | collective-permute-start | bytes 1376264 | tf_op jit(solution)/shard_map/ppermute | solution.py:71
  112.2 16.8 %collective-permute-start.32 = (bf16[128,1792]{1,0:T(8,128)(2,1)S(1)}, bf16[128,1792]{1,0:T(8,128)(2,1)S(1)}, u32[]{:S(2)}, u32[]{:S(2)}) collective-permute-start(bf16[128,1792]{1,0:T(8,128)(2,1)S(1)} %add_convert_fusion.1), channel_id=1, source_target_pairs={{0,4},{2,6},{4,0},{6,2},{8,12},{10,14},{12,8},{14,10},{16,20},{18,... | collective-permute-start | bytes 1376264 | tf_op jit(solution)/shard_map/ppermute | solution.py:71
  114.0 15.0 %collective-permute-start.33 = (bf16[128,1792]{1,0:T(8,128)(2,1)S(1)}, bf16[128,1792]{1,0:T(8,128)(2,1)S(1)}, u32[]{:S(2)}, u32[]{:S(2)}) collective-permute-start(bf16[128,1792]{1,0:T(8,128)(2,1)S(1)} %add_convert_fusion), channel_id=1, source_target_pairs={{0,8},{2,10},{4,12},{6,14},{8,0},{10,2},{12,4},{14,6},{16,24},{18,... | collective-permute-start | bytes 1376264 | tf_op jit(solution)/shard_map/ppermute | solution.py:71
  125.9 10.3 %collective-permute-start.25 = (f32[512,384]{1,0:T(8,128)}, f32[512,384]{1,0:T(8,128)}, u32[]{:S(2)}, u32[]{:S(2)}) collective-permute-start(f32[512,384]{1,0:T(8,128)} %get-tuple-element.121.refs_14_.refs_3_), channel_id=1, source_target_pairs={{0,1},{1,0},{2,3},{3,2},{4,5},{5,4},{6,7},{7,6},{8,9},{9,8},{10,11... | collective-permute-start | bytes 2359304 | tf_op jit(solution)/shard_map/ppermute | solution.py:75
  126.0 20.3 %collective-permute-start.29 = (bf16[64,1792]{1,0:T(8,128)(2,1)}, bf16[64,1792]{1,0:T(8,128)(2,1)}, u32[]{:S(2)}, u32[]{:S(2)}) collective-permute-start(bf16[64,1792]{1,0:T(8,128)(2,1)} %get-tuple-element.135), channel_id=1, source_target_pairs={{0,2},{2,0},{4,6},{6,4},{8,10},{10,8},{12,14},{14,12},{16,18},{18,... | collective-permute-start | bytes 688136 | tf_op jit(solution)/shard_map/ppermute | solution.py:71
  127.5 18.8 %collective-permute-start.30 = (bf16[64,1792]{1,0:T(8,128)(2,1)}, bf16[64,1792]{1,0:T(8,128)(2,1)}, u32[]{:S(2)}, u32[]{:S(2)}) collective-permute-start(bf16[64,1792]{1,0:T(8,128)(2,1)} %get-tuple-element.136), channel_id=1, source_target_pairs={{0,4},{2,6},{4,0},{6,2},{8,12},{10,14},{12,8},{14,10},{16,20},{18,... | collective-permute-start | bytes 688136 | tf_op jit(solution)/shard_map/ppermute | solution.py:71
  133.0 13.6 %collective-permute-start.36 = (bf16[64,1792]{1,0:T(8,128)(2,1)}, bf16[64,1792]{1,0:T(8,128)(2,1)}, u32[]{:S(2)}, u32[]{:S(2)}) collective-permute-start(bf16[64,1792]{1,0:T(8,128)(2,1)} %get-tuple-element.184), channel_id=1, source_target_pairs={{0,16},{2,18},{4,20},{6,22},{8,24},{10,26},{12,28},{14,30},{16,0},... | collective-permute-start | bytes 688136 | tf_op jit(solution)/shard_map/ppermute | solution.py:71
  134.3 12.5 %collective-permute-start.34 = (bf16[64,1792]{1,0:T(8,128)(2,1)}, bf16[64,1792]{1,0:T(8,128)(2,1)}, u32[]{:S(2)}, u32[]{:S(2)}) collective-permute-start(bf16[64,1792]{1,0:T(8,128)(2,1)} %get-tuple-element.185), channel_id=1, source_target_pairs={{0,8},{2,10},{4,12},{6,14},{8,0},{10,2},{12,4},{14,6},{16,24},{18,... | collective-permute-start | bytes 688136 | tf_op jit(solution)/shard_map/ppermute | solution.py:71
  136.3 10.5 %collective-permute-start.35 = (bf16[64,1792]{1,0:T(8,128)(2,1)}, bf16[64,1792]{1,0:T(8,128)(2,1)}, u32[]{:S(2)}, u32[]{:S(2)}) collective-permute-start(bf16[64,1792]{1,0:T(8,128)(2,1)} %get-tuple-element.186), channel_id=1, source_target_pairs={{0,6},{2,4},{4,2},{6,0},{8,14},{10,12},{12,10},{14,8},{16,22},{18,... | collective-permute-start | bytes 688136 | tf_op jit(solution)/shard_map/ppermute | solution.py:71
  146.8 8.1 %collective-permute-start.37 = (bf16[128,768]{1,0:T(8,128)(2,1)}, bf16[128,768]{1,0:T(8,128)(2,1)}, u32[]{:S(2)}, u32[]{:S(2)}) collective-permute-start(bf16[128,768]{1,0:T(8,128)(2,1)} %get-tuple-element.149), channel_id=1, source_target_pairs={{0,2},{2,0},{4,6},{6,4},{8,10},{10,8},{12,14},{14,12},{16,18},{18,... | collective-permute-start | bytes 589832 | tf_op jit(solution)/shard_map/ppermute | solution.py:71
  148.4 12.8 %collective-permute-start.28 = (bf16[128,768]{1,0:T(8,128)(2,1)}, bf16[128,768]{1,0:T(8,128)(2,1)S(1)}, u32[]{:S(2)}, u32[]{:S(2)}) collective-permute-start(bf16[128,768]{1,0:T(8,128)(2,1)} %get-tuple-element.130.refs_8_), channel_id=1, source_target_pairs={{0,2},{2,0},{4,6},{6,4},{8,10},{10,8},{12,14},{14,12},{16,18},{18,... | collective-permute-start | bytes 589832 | tf_op jit(solution)/shard_map/ppermute | solution.py:71
  149.9 8.2 %collective-permute-start.40 = (bf16[64,768]{1,0:T(8,128)(2,1)}, bf16[64,768]{1,0:T(8,128)(2,1)S(1)}, u32[]{:S(2)}, u32[]{:S(2)}) collective-permute-start(bf16[64,768]{1,0:T(8,128)(2,1)} %get-tuple-element.152), channel_id=1, source_target_pairs={{0,16},{2,18},{4,20},{6,22},{8,24},{10,26},{12,28},{14,30},{16,0},... | collective-permute-start | bytes 294920 | tf_op jit(solution)/shard_map/ppermute | solution.py:71
  150.3 7.7 %collective-permute-start.41 = (bf16[64,768]{1,0:T(8,128)(2,1)}, bf16[64,768]{1,0:T(8,128)(2,1)S(1)}, u32[]{:S(2)}, u32[]{:S(2)}) collective-permute-start(bf16[64,768]{1,0:T(8,128)(2,1)} %get-tuple-element.153), channel_id=1, source_target_pairs={{0,4},{2,6},{4,0},{6,2},{8,12},{10,14},{12,8},{14,10},{16,20},{18,... | collective-permute-start | bytes 294920 | tf_op jit(solution)/shard_map/ppermute | solution.py:71
  156.8 6.8 %collective-permute-start.38 = (bf16[128,768]{1,0:T(8,128)(2,1)S(1)}, bf16[128,768]{1,0:T(8,128)(2,1)S(1)}, u32[]{:S(2)}, u32[]{:S(2)}) collective-permute-start(bf16[128,768]{1,0:T(8,128)(2,1)S(1)} %add_convert_fusion.6), channel_id=1, source_target_pairs={{0,4},{2,6},{4,0},{6,2},{8,12},{10,14},{12,8},{14,10},{16,20},{18,... | collective-permute-start | bytes 589832 | tf_op jit(solution)/shard_map/ppermute | solution.py:71
  159.1 5.7 %collective-permute-start.42 = (bf16[128,768]{1,0:T(8,128)(2,1)S(1)}, bf16[128,768]{1,0:T(8,128)(2,1)S(1)}, u32[]{:S(2)}, u32[]{:S(2)}) collective-permute-start(bf16[128,768]{1,0:T(8,128)(2,1)S(1)} %add_convert_fusion.5), channel_id=1, source_target_pairs={{0,8},{2,10},{4,12},{6,14},{8,0},{10,2},{12,4},{14,6},{16,24},{18,... | collective-permute-start | bytes 589832 | tf_op jit(solution)/shard_map/ppermute | solution.py:71
  159.2 12.1 %collective-permute-start.26 = (bf16[64,768]{1,0:T(8,128)(2,1)}, bf16[64,768]{1,0:T(8,128)(2,1)S(1)}, u32[]{:S(2)}, u32[]{:S(2)}) collective-permute-start(bf16[64,768]{1,0:T(8,128)(2,1)} %get-tuple-element.127), channel_id=1, source_target_pairs={{0,2},{2,0},{4,6},{6,4},{8,10},{10,8},{12,14},{14,12},{16,18},{18,... | collective-permute-start | bytes 294920 | tf_op jit(solution)/shard_map/ppermute | solution.py:71
  160.3 11.2 %collective-permute-start.27 = (bf16[64,768]{1,0:T(8,128)(2,1)}, bf16[64,768]{1,0:T(8,128)(2,1)S(1)}, u32[]{:S(2)}, u32[]{:S(2)}) collective-permute-start(bf16[64,768]{1,0:T(8,128)(2,1)} %get-tuple-element.128), channel_id=1, source_target_pairs={{0,4},{2,6},{4,0},{6,2},{8,12},{10,14},{12,8},{14,10},{16,20},{18,... | collective-permute-start | bytes 294920 | tf_op jit(solution)/shard_map/ppermute | solution.py:71
  165.9 5.5 %collective-permute-start.39 = (bf16[64,768]{1,0:T(8,128)(2,1)S(1)}, bf16[64,768]{1,0:T(8,128)(2,1)S(1)}, u32[]{:S(2)}, u32[]{:S(2)}) collective-permute-start(bf16[64,768]{1,0:T(8,128)(2,1)S(1)} %get-tuple-element.189), channel_id=1, source_target_pairs={{0,8},{2,10},{4,12},{6,14},{8,0},{10,2},{12,4},{14,6},{16,24},{18,... | collective-permute-start | bytes 294920 | tf_op jit(solution)/shard_map/ppermute | solution.py:71
  166.0 5.6 %collective-permute-start.44 = (bf16[64,768]{1,0:T(8,128)(2,1)S(1)}, bf16[64,768]{1,0:T(8,128)(2,1)S(1)}, u32[]{:S(2)}, u32[]{:S(2)}) collective-permute-start(bf16[64,768]{1,0:T(8,128)(2,1)S(1)} %get-tuple-element.190), channel_id=1, source_target_pairs={{0,16},{2,18},{4,20},{6,22},{8,24},{10,26},{12,28},{14,30},{16,0},... | collective-permute-start | bytes 294920 | tf_op jit(solution)/shard_map/ppermute | solution.py:71
  167.8 5.5 %collective-permute-start.43 = (bf16[64,768]{1,0:T(8,128)(2,1)S(1)}, bf16[64,768]{1,0:T(8,128)(2,1)S(1)}, u32[]{:S(2)}, u32[]{:S(2)}) collective-permute-start(bf16[64,768]{1,0:T(8,128)(2,1)S(1)} %get-tuple-element.191), channel_id=1, source_target_pairs={{0,6},{2,4},{4,2},{6,0},{8,14},{10,12},{12,10},{14,8},{16,22},{18,... | collective-permute-start | bytes 294920 | tf_op jit(solution)/shard_map/ppermute | solution.py:71
  171.4 3.6 %collective-permute-start.46 = (f32[64,1792]{1,0:T(8,128)S(1)}, f32[64,1792]{1,0:T(8,128)S(1)}, u32[]{:S(2)}, u32[]{:S(2)}) collective-permute-start(f32[64,1792]{1,0:T(8,128)S(1)} %convert_add_fusion.refs_3_), channel_id=1, source_target_pairs={{0,1},{1,0},{2,3},{3,2},{4,5},{5,4},{6,7},{7,6},{8,9},{9,8},{10,11... | collective-permute-start | bytes 1376264 | tf_op jit(solution)/shard_map/ppermute | solution.py:75
  179.2 4.8 %collective-permute-start.50 = (f32[8,1024]{1,0:T(8,128)S(1)}, f32[8,1024]{1,0:T(8,128)S(1)}, u32[]{:S(2)}, u32[]{:S(2)}) collective-permute-start(f32[8,1024]{1,0:T(8,128)S(1)} %get-tuple-element.167), channel_id=1, source_target_pairs={{0,6},{2,4},{4,2},{6,0},{8,14},{10,12},{12,10},{14,8},{16,22},{18,... | collective-permute-start | bytes 98312 | tf_op jit(solution)/shard_map/ppermute | solution.py:71
  181.2 3.9 %collective-permute-start.49 = (f32[8,1024]{1,0:T(8,128)S(1)}, f32[8,1024]{1,0:T(8,128)S(1)}, u32[]{:S(2)}, u32[]{:S(2)}) collective-permute-start(f32[8,1024]{1,0:T(8,128)S(1)} %get-tuple-element.167), channel_id=1, source_target_pairs={{0,4},{2,6},{4,0},{6,2},{8,12},{10,14},{12,8},{14,10},{16,20},{18,... | collective-permute-start | bytes 98312 | tf_op jit(solution)/shard_map/ppermute | solution.py:71
  181.7 3.9 %collective-permute-start.48 = (f32[8,1024]{1,0:T(8,128)S(1)}, f32[8,1024]{1,0:T(8,128)S(1)}, u32[]{:S(2)}, u32[]{:S(2)}) collective-permute-start(f32[8,1024]{1,0:T(8,128)S(1)} %get-tuple-element.167), channel_id=1, source_target_pairs={{0,2},{2,0},{4,6},{6,4},{8,10},{10,8},{12,14},{14,12},{16,18},{18,... | collective-permute-start | bytes 98312 | tf_op jit(solution)/shard_map/ppermute | solution.py:71
  185.7 5.8 %collective-permute-start.53 = (f32[8,1024]{1,0:T(8,128)S(1)}, f32[8,1024]{1,0:T(8,128)S(1)}, u32[]{:S(2)}, u32[]{:S(2)}) collective-permute-start(f32[8,1024]{1,0:T(8,128)S(1)} %add_add_fusion.1), channel_id=1, source_target_pairs={{0,24},{2,26},{4,28},{6,30},{8,16},{10,18},{12,20},{14,22},{16,8},... | collective-permute-start | bytes 98312 | tf_op jit(solution)/shard_map/ppermute | solution.py:71
  188.2 4.8 %collective-permute-start.52 = (f32[8,1024]{1,0:T(8,128)S(1)}, f32[8,1024]{1,0:T(8,128)S(1)}, u32[]{:S(2)}, u32[]{:S(2)}) collective-permute-start(f32[8,1024]{1,0:T(8,128)S(1)} %add_add_fusion.1), channel_id=1, source_target_pairs={{0,16},{2,18},{4,20},{6,22},{8,24},{10,26},{12,28},{14,30},{16,0},... | collective-permute-start | bytes 98312 | tf_op jit(solution)/shard_map/ppermute | solution.py:71
  188.2 4.8 %collective-permute-start.51 = (f32[8,1024]{1,0:T(8,128)S(1)}, f32[8,1024]{1,0:T(8,128)S(1)}, u32[]{:S(2)}, u32[]{:S(2)}) collective-permute-start(f32[8,1024]{1,0:T(8,128)S(1)} %add_add_fusion.1), channel_id=1, source_target_pairs={{0,8},{2,10},{4,12},{6,14},{8,0},{10,2},{12,4},{14,6},{16,24},{18,... | collective-permute-start | bytes 98312 | tf_op jit(solution)/shard_map/ppermute | solution.py:71
  (63 other events, 900.3 us)
where the time goes:
time: 195 us
  Pallas kernels  70.2 us (36%)
  starting transfers between devices  49.8 us (26%)
  waiting for transfers between devices  49.1 us (25%)
  local copies, waits for them, and re-layouts  15.6 us (8%)
  other arithmetic  8.46 us (4%)
    ppermute x39, starting transfers between devices, flip(): lax.ppermute(array, 'dp', [(i, i ^ mask) for i in range(lax.axis_size('dp...  46.9 us
    ppermute x39, waiting for transfers between devices, flip(): lax.ppermute(array, 'dp', [(i, i ^ mask) for i in range(lax.axis_size('dp...  42.6 us
    pallas_call x2, Pallas kernels, pixel_back(): pl.pallas_call(functools.partial(pixel_back_kernel, scale, turn, turns),...  21.4 us
    pallas_call x1, Pallas kernels, chain(): pl.pallas_call(functools.partial(chain_kernel, len(blocks), layout, len(o...  18.2 us
    unnamed x114, local copies, waits for them, and re-layouts  12.2 us
    pallas_call x1, Pallas kernels, attend(): pl.pallas_call(functools.partial(attend_kernel, len(blocks), layout, scal...  9.11 us
    pallas_call x1, Pallas kernels, query_back(): pl.pallas_call(functools.partial(query_back_kernel, len(blocks), layout,...  8.91 us
    ppermute x15, waiting for transfers between devices, trade(): return lax.ppermute(array, 'seq', swap)  6.5 us
  transfers between devices with their start and end apart: 54, of which 26 were waited for; matrix products, arithmetic and copies ran while one was open for 6% of the time, Pallas kernels for 23%

commit v1 on v0

--- a/solution.py
+++ b/solution.py
@@ -39,7 +39,7 @@
 remote = pl.BlockSpec(memory_space=pl.ANY)
 scalars = pl.BlockSpec(memory_space=pltpu.SMEM)
 params = pltpu.CompilerParams(vmem_limit_bytes=40 * 2**20)
-params_most = pltpu.CompilerParams(vmem_limit_bytes=56 * 2**20)
+params_most = pltpu.CompilerParams(vmem_limit_bytes=52 * 2**20)
 params_all = pltpu.CompilerParams(vmem_limit_bytes=63 * 2**20)
 
 
@@ -688,13 +688,9 @@
     if turn > 0:
         value = value + score_before[...]
     score_pix[...] = value * scale if turn == turns - 1 else value
-    lane = lax.broadcasted_iota(jnp.int32, (feats, 128), 1)
-    both = jnp.where(
-        lane == 0,
-        jnp.sum(slope[...], axis=-1, keepdims=True),
-        jnp.sum(shift[...], axis=-1, keepdims=True),
-    )
-    sums[...] = both + sums_before[...] if turn > 0 else both
+    sums[...] = sums_before[...] if turn > 0 else jnp.zeros_like(sums)
+    for row, array in ((6, slope), (7, shift)):
+        sums[row : row + 1, pl.ds(0, main + rest)] += jnp.sum(jnp.transpose(array[...]), axis=0, keepdims=True)
 
     @pl.loop(0, count // (2 * step))
     def _(i):
@@ -707,7 +703,7 @@
     held = pltpu.VMEM((feats, count // turns), single)
     return pl.pallas_call(
         functools.partial(pixel_back_kernel, scale, turn, turns),
-        out_shape=[shape((rows, main + rest), single), shape((feats, 128), single), shape(pixels.shape, single)],
+        out_shape=[shape((rows, main + rest), single), shape((8, 2 * rows), single), shape(pixels.shape, single)],
         in_specs=[whole] * 3 + [remote, whole, remote, whole, whole] + [whole, whole, remote][: len(before)],
         out_specs=[whole, whole, remote],
         scratch_shapes=[
@@ -717,8 +713,8 @@
             pltpu.VMEM((rows, count // turns), half),
             pltpu.VMEM((main + 16, rows), half),
             pltpu.VMEM((main + 16, rows), half),
-            pltpu.VMEM((feats, 128), single),
-            pltpu.VMEM((feats, 128), single),
+            pltpu.VMEM((main + rest, 128), single),
+            pltpu.VMEM((main + rest, 128), single),
             pltpu.SemaphoreType.DMA((2 + count // turns // 512,)),
         ],
         input_output_aliases={10: 2} if before else {},
@@ -956,8 +952,7 @@
     early = sum_own(early_terms, early_got)
     late = sum_own(late_terms, send_third(late_terms, send_second(late_terms, send_first(late_terms))))
 
-    norm_terms = jnp.pad(jnp.transpose(pixel_sums[:, :2]), ((6, 0), (0, width - feats)))
-    vector_terms = chain_sums + query_sums + norm_terms
+    vector_terms = chain_sums + query_sums + pixel_sums
     vector_terms = vector_terms + trade(vector_terms)
     square_grad, square_first_new, square_second_new, square_u, *rest_outs = moments(
         spot, (late, trade(late)), (early, trade(early)), vector_terms, square, pixel

time: 195 us -> 194 us (level)
    unnamed x114 -> x124, local copies, waits for them, and re-layouts: 12.2 us -> 15 us
  transfers between devices with their start and end apart: 54 -> 54, of which waited for: 26 -> 26; matrix products, arithmetic and copies ran while one was open for 6% -> 5% of each run, Pallas kernels for 23% -> 23%
where the time goes in v1:
time: 194 us
  Pallas kernels  68.7 us (35%)
  starting transfers between devices  49.8 us (26%)
  waiting for transfers between devices  49 us (25%)
  local copies, waits for them, and re-layouts  16.4 us (8%)
  other arithmetic  8.46 us (4%)
    ppermute x39, starting transfers between devices, flip(): lax.ppermute(array, 'dp', [(i, i ^ mask) for i in range(lax.axis_size('dp...  46.9 us
    ppermute x39, waiting for transfers between devices, flip(): lax.ppermute(array, 'dp', [(i, i ^ mask) for i in range(lax.axis_size('dp...  44.4 us
    pallas_call x2, Pallas kernels, pixel_back(): pl.pallas_call(functools.partial(pixel_back_kernel, scale, turn, turns),...  19.9 us
    pallas_call x1, Pallas kernels, chain(): pl.pallas_call(functools.partial(chain_kernel, len(blocks), layout, len(o...  18.3 us
    unnamed x124, local copies, waits for them, and re-layouts  15 us
    pallas_call x1, Pallas kernels, attend(): pl.pallas_call(functools.partial(attend_kernel, len(blocks), layout, scal...  9.11 us
    pallas_call x1, Pallas kernels, query_back(): pl.pallas_call(functools.partial(query_back_kernel, len(blocks), layout,...  8.9 us
    pallas_call x1, Pallas kernels, norm_pixels(): pl.pallas_call(pixel_kernel, out_shape=[shape((main + rest, count), half)...  5.62 us
  transfers between devices with their start and end apart: 54, of which 26 were waited for; matrix products, arithmetic and copies ran while one was open for 5% of the time, Pallas kernels for 23%

profile of v1, /device:TPU:0, one launch (start us, length us, event | category | flops | bytes accessed | tf_op | source)
XLA Modules:
  0.0 193.7 jit_solution(4951458139170260063)
XLA Ops:
  0.8 1.2 copy-done.9
  3.5 3.0 %collective-permute-start.4 = (bf16[64,2560]{1,0:T(8,128)(2,1)S(1)}, bf16[64,2560]{1,0:T(8,128)(2,1)S(1)}, u32[]{:S(2)}, u32[]{:S(2)}) collective-permute-start(bf16[64,2560]{1,0:T(8,128)(2,1)S(1)} %pack.1.refs_0_), channel_id=1, source_target_pairs={{0,2},{2,0},{4,6},{6,4},{8,10},{10,8},{12,14},{14,12},{16,18},{18,... | collective-permute-start | bytes 983048 | tf_op jit(solution)/shard_map/ppermute | solution.py:71
  6.5 1.5 collective-permute-start.3
  8.0 2.0 %collective-permute-start.1 = (bf16[64,2560]{1,0:T(8,128)(2,1)S(1)}, bf16[64,2560]{1,0:T(8,128)(2,1)S(1)}, u32[]{:S(2)}, u32[]{:S(2)}) collective-permute-start(bf16[64,2560]{1,0:T(8,128)(2,1)S(1)} %pack.1.refs_0_), channel_id=1, source_target_pairs={{0,8},{2,10},{4,12},{6,14},{8,0},{10,2},{12,4},{14,6},{16,24},{18,... | collective-permute-start | bytes 983048 | tf_op jit(solution)/shard_map/ppermute | solution.py:71
  10.1 2.6 %collective-permute-start = (bf16[64,2560]{1,0:T(8,128)(2,1)S(1)}, bf16[64,2560]{1,0:T(8,128)(2,1)S(1)}, u32[]{:S(2)}, u32[]{:S(2)}) collective-permute-start(bf16[64,2560]{1,0:T(8,128)(2,1)S(1)} %pack.1.refs_0_), channel_id=1, source_target_pairs={{0,16},{2,18},{4,20},{6,22},{8,24},{10,26},{12,28},{14,30},{16,0},... | collective-permute-start | bytes 983048 | tf_op jit(solution)/shard_map/ppermute | solution.py:71
  13.0 2.2 %copy-done.3 = f32[1,4096,261]{1,0,2:T(1,128)S(1)} copy-done((f32[1,4096,261]{1,0,2:T(1,128)S(1)}, f32[1,4096,261]{1,0,2:T(1,128)}, u32[]{:S(2)}) %copy-start.3) | copy-done | bytes 4276248
  15.2 5.6 %norm_pixels.1 = (bf16[384,4096]{1,0:T(8,128)(2,1)S(1)}, f32[2,4096]{1,0:T(2,128)S(1)}) custom-call(f32[261,1,4096]{2,1,0:T(1,128)S(1)} %bitcast.30, f32[261,1]{1,0:T(8,128)S(1)} %copy.52.gain.refs_6_, f32[261,1]{1,0:T(8,128)S(1)} %copy.53.shift), custom_call_target="tpu_custom_call" | custom-call | flops 7699999744 | bytes 1024 | tf_op jit(solution)/shard_map/norm_pixels/pallas_call | solution.py:356
  20.8 1.7 collective-permute-done.2.refs_3_.refs_0_
  22.5 1.3 collective-permute-done.1.refs_2_.refs_1_
  23.8 2.6 %collective-permute-done.refs_1_.refs_2_ = bf16[64,2560]{1,0:T(8,128)(2,1)S(1)} collective-permute-done((bf16[64,2560]{1,0:T(8,128)(2,1)S(1)}, bf16[64,2560]{1,0:T(8,128)(2,1)S(1)}, u32[]{:S(2)}, u32[]{:S(2)}) %collective-permute-start) | collective-permute-done | bytes 327712 | tf_op jit(solution)/shard_map/ppermute | solution.py:71
  27.2 1.5 collective-permute-start.10
  28.7 1.5 collective-permute-start.8
  32.4 7.6 %collective-permute-done.6.refs_0_.refs_2_ = bf16[128,2560]{1,0:T(8,128)(2,1)S(1)} collective-permute-done((bf16[128,2560]{1,0:T(8,128)(2,1)S(1)}, bf16[128,2560]{1,0:T(8,128)(2,1)S(1)}, u32[]{:S(2)}, u32[]{:S(2)}) %collective-permute-start.6) | collective-permute-done | bytes 655392 | tf_op jit(solution)/shard_map/ppermute | solution.py:71
  40.0 1.3 collective-permute-done.10.refs_2_.refs_6_
  41.4 1.7 collective-permute-done.8.refs_1_.refs_4_
  44.4 1.5 collective-permute-start.14
  45.9 10.3 %collective-permute-done.12.refs_8_ = bf16[64,2560]{1,0:T(8,128)(2,1)S(1)} collective-permute-done((bf16[64,2560]{1,0:T(8,128)(2,1)S(1)}, bf16[64,2560]{1,0:T(8,128)(2,1)S(1)}, u32[]{:S(2)}, u32[]{:S(2)}) %collective-permute-start.12) | collective-permute-done | bytes 327712 | tf_op jit(solution)/shard_map/ppermute | solution.py:71
  59.4 1.3 collective-permute-done.13.refs_9_
  61.2 9.1 %attend.1 = (bf16[512,1024]{1,0:T(8,128)(2,1)S(1)}, bf16[512,384]{1,0:T(8,128)(2,1)S(1)}, f32[512,384]{1,0:T(8,128)S(1)}) custom-call(s32[2]{0:T(128)S(1)} %pad_add_fusion.spot.refs_0_, bf16[384,2560]{1,0:T(8,128)(2,1)S(1)} %stack.15.refs_0_, bf16[384,2560]{1,0:T(8,128)(2,1)S(1)} %collective-permute-done.5.refs_1_, ...), custom_call_target="tpu_custom_call" | custom-call | flops 12099999744 | bytes 1024 | tf_op jit(solution)/shard_map/attend/pallas_call | solution.py:438
  73.7 18.3 %chain.1 = (f32[256,1024]{1,0:T(8,128)}, f32[256,1024]{1,0:T(8,128)S(1)}, bf16[512,384]{1,0:T(8,128)(2,1)S(1)}, f32[512,128]{1,0:T(8,128)S(1)}, f32[8,1024]{1,0:...) custom-call(s32[2]{0:T(128)S(1)} %pad_add_fusion.spot.refs_0_, ...), custom_call_target="tpu_custom_call" | custom-call | flops 18699999232 | bytes 1024 | tf_op jit(solution)/shard_map/chain/pallas_call | solution.py:586
  94.3 1.5 collective-permute-start.23
  96.8 1.3 collective-permute-start.31
  98.1 9.3 %pixel_back.2 = (f32[512,384]{1,0:T(8,128)}, f32[8,1024]{1,0:T(8,128)S(1)}, f32[261,1,4096]{2,1,0:T(1,128)}) custom-call(bf16[512,384]{1,0:T(8,128)(2,1)S(1)} %get-tuple-element.110.refs_0_, bf16[512,384]{1,0:T(8,128)(2,1)S(1)} %get-tuple-element.111.refs_1_, f32[512,128]{1,0:T(8,128)S(1)} %get-tuple-element.112.refs_2_, bf16[384,4096]{1,0:T(8,128)(2,1)} %copy-done.44, ...), custom_call_target="tpu_custom_call" | custom-call | flops 9900000256 | bytes 1024 | tf_op jit(solution)/shard_map/pixel_back/pallas_call | solution.py:704
  108.2 1.5 collective-permute-done.22.refs_0_
  114.6 10.5 %pixel_back.3 = (f32[512,384]{1,0:T(8,128)}, f32[8,1024]{1,0:T(8,128)S(1)}, f32[261,1,4096]{2,1,0:T(1,128)}) custom-call(bf16[512,384]{1,0:T(8,128)(2,1)S(1)} %copy-done.48, bf16[512,384]{1,0:T(8,128)(2,1)S(1)} %copy-done.50, f32[512,128]{1,0:T(8,128)S(1)} %copy-done.52, bf16[384,4096]{1,0:T(8,128)(2,1)} %copy-done.44, ...), custom_call_target="tpu_custom_call", output_to_operand_aliasing={{2}: (10, {})} | custom-call | flops 9900000256 | bytes 1024 | tf_op jit(solution)/shard_map/pixel_back/pallas_call | solution.py:704
  125.2 1.5 collective-permute-start.29
  126.7 1.5 collective-permute-start.30
  129.8 2.5 %add_convert_fusion.2 = (bf16[64,1792]{1,0:T(8,128)(2,1)}, bf16[64,1792]{1,0:T(8,128)(2,1)}, bf16[64,1792]{1,0:T(8,128)(2,1)}) fusion(bf16[64,1792]{1,0:T(8,128)(2,1)S(1)} %get-tuple-element.148, bf16[128,1792]{1,0:T(8,128)(2,1)} %get-tuple-element.147, bf16[128,1792]{1,0:T(8,128)(2,1)} %get-tuple-element.145, bf16[128,1792]{1,0:T(8,128)(2,1)} %get-tuple-element.144, ...), kind=kLoop, calls=%fused_computation.3 | loop fusion | flops 2064384 | bytes 2752512 | tf_op jit(solution)/shard_map/convert_element_type | solution.py:289
  132.2 1.2 collective-permute-start.36
  133.5 2.0 %collective-permute-start.34 = (bf16[64,1792]{1,0:T(8,128)(2,1)}, bf16[64,1792]{1,0:T(8,128)(2,1)}, u32[]{:S(2)}, u32[]{:S(2)}) collective-permute-start(bf16[64,1792]{1,0:T(8,128)(2,1)} %get-tuple-element.185), channel_id=1, source_target_pairs={{0,8},{2,10},{4,12},{6,14},{8,0},{10,2},{12,4},{14,6},{16,24},{18,... | collective-permute-start | bytes 688136 | tf_op jit(solution)/shard_map/ppermute | solution.py:71
  136.5 8.9 %query_back.1 = (f32[256,1024]{1,0:T(8,128)}, f32[8,1024]{1,0:T(8,128)}, bf16[128,768]{1,0:T(8,128)(2,1)}, bf16[64,768]{1,0:T(8,128)(2,1)}, bf16[64,768]{1,0:T(8...) custom-call(s32[2]{0:T(128)} %copy-done.42, ...), custom_call_target="tpu_custom_call" | custom-call | flops 7699999744 | bytes 1024 | tf_op jit(solution)/shard_map/query_back/pallas_call | solution.py:774
  146.6 1.4 collective-permute-start.28
  149.4 4.6 %collective-permute-done.37 = bf16[128,768]{1,0:T(8,128)(2,1)S(1)} collective-permute-done((bf16[128,768]{1,0:T(8,128)(2,1)}, bf16[128,768]{1,0:T(8,128)(2,1)S(1)}, u32[]{:S(2)}, u32[]{:S(2)}) %collective-permute-start.37) | collective-permute-done | bytes 196640 | tf_op jit(solution)/shard_map/ppermute | solution.py:71
  155.0 1.3 collective-permute-start.38
  159.5 2.2 %collective-permute-done.38 = bf16[128,768]{1,0:T(8,128)(2,1)S(1)} collective-permute-done((bf16[128,768]{1,0:T(8,128)(2,1)S(1)}, bf16[128,768]{1,0:T(8,128)(2,1)S(1)}, u32[]{:S(2)}, u32[]{:S(2)}) %collective-permute-start.38) | collective-permute-done | bytes 196640 | tf_op jit(solution)/shard_map/ppermute | solution.py:71
  161.7 1.3 collective-permute-done.42
  164.2 1.7 collective-permute-start.44
  166.0 2.0 %collective-permute-start.43 = (bf16[64,768]{1,0:T(8,128)(2,1)S(1)}, bf16[64,768]{1,0:T(8,128)(2,1)S(1)}, u32[]{:S(2)}, u32[]{:S(2)}) collective-permute-start(bf16[64,768]{1,0:T(8,128)(2,1)S(1)} %get-tuple-element.191), channel_id=1, source_target_pairs={{0,6},{2,4},{4,2},{6,0},{8,14},{10,12},{12,10},{14,8},{16,22},{18,... | collective-permute-start | bytes 294920 | tf_op jit(solution)/shard_map/ppermute | solution.py:71
  168.0 1.5 convert_add_fusion.refs_3_
  169.8 1.7 collective-permute-done.43
  174.1 4.1 %moments.1 = (f32[4,64,1024]{2,1,0:T(8,128)}, f32[4,64,1024]{2,1,0:T(8,128)}, f32[4,64,1024]{2,1,0:T(8,128)}, f32[4,64,1024]{2,1,0:T(8,128)S(1)}, f32[2,64,261]{...) custom-call(s32[2]{0:T(128)S(1)} %copy-done.43, ...), custom_call_target="tpu_custom_call" | custom-call | flops 5500000256 | bytes 1024 | tf_op jit(solution)/shard_map/moments/pallas_call | solution.py:837
  178.2 2.0 %collective-permute-start.50 = (f32[8,1024]{1,0:T(8,128)S(1)}, f32[8,1024]{1,0:T(8,128)S(1)}, u32[]{:S(2)}, u32[]{:S(2)}) collective-permute-start(f32[8,1024]{1,0:T(8,128)S(1)} %get-tuple-element.167), channel_id=1, source_target_pairs={{0,6},{2,4},{4,2},{6,0},{8,14},{10,12},{12,10},{14,8},{16,22},{18,... | collective-permute-start | bytes 98312 | tf_op jit(solution)/shard_map/ppermute | solution.py:71
  181.7 1.3 collective-permute-done.50
  184.7 2.5 %collective-permute-start.53 = (f32[8,1024]{1,0:T(8,128)S(1)}, f32[8,1024]{1,0:T(8,128)S(1)}, u32[]{:S(2)}, u32[]{:S(2)}) collective-permute-start(f32[8,1024]{1,0:T(8,128)S(1)} %add_add_fusion.1), channel_id=1, source_target_pairs={{0,24},{2,26},{4,28},{6,30},{8,16},{10,18},{12,20},{14,22},{16,8},... | collective-permute-start | bytes 98312 | tf_op jit(solution)/shard_map/ppermute | solution.py:71
  187.2 1.9 collective-permute-start.51
  189.1 1.3 collective-permute-done.53
  190.5 1.6 collective-permute-done.52
  192.1 1.6 apply.1
  (218 shorter events, 38.4 us)
Async XLA Ops:
  3.5 26.7 %collective-permute-start.4 = (bf16[64,2560]{1,0:T(8,128)(2,1)S(1)}, bf16[64,2560]{1,0:T(8,128)(2,1)S(1)}, u32[]{:S(2)}, u32[]{:S(2)}) collective-permute-start(bf16[64,2560]{1,0:T(8,128)(2,1)S(1)} %pack.1.refs_0_), channel_id=1, source_target_pairs={{0,2},{2,0},{4,6},{6,4},{8,10},{10,8},{12,14},{14,12},{16,18},{18,... | collective-permute-start | bytes 983048 | tf_op jit(solution)/shard_map/ppermute | solution.py:71
  6.5 23.7 %collective-permute-start.3 = (bf16[64,2560]{1,0:T(8,128)(2,1)S(1)}, bf16[64,2560]{1,0:T(8,128)(2,1)S(1)}, u32[]{:S(2)}, u32[]{:S(2)}) collective-permute-start(bf16[64,2560]{1,0:T(8,128)(2,1)S(1)} %pack.1.refs_0_), channel_id=1, source_target_pairs={{0,4},{2,6},{4,0},{6,2},{8,12},{10,14},{12,8},{14,10},{16,20},{18,... | collective-permute-start | bytes 983048 | tf_op jit(solution)/shard_map/ppermute | solution.py:71
  8.0 14.5 %collective-permute-start.2 = (bf16[64,2560]{1,0:T(8,128)(2,1)S(1)}, bf16[64,2560]{1,0:T(8,128)(2,1)S(1)}, u32[]{:S(2)}, u32[]{:S(2)}) collective-permute-start(bf16[64,2560]{1,0:T(8,128)(2,1)S(1)} %pack.1.refs_0_), channel_id=1, source_target_pairs={{0,6},{2,4},{4,2},{6,0},{8,14},{10,12},{12,10},{14,8},{16,22},{18,... | collective-permute-start | bytes 983048 | tf_op jit(solution)/shard_map/ppermute | solution.py:71
  8.0 15.8 %collective-permute-start.1 = (bf16[64,2560]{1,0:T(8,128)(2,1)S(1)}, bf16[64,2560]{1,0:T(8,128)(2,1)S(1)}, u32[]{:S(2)}, u32[]{:S(2)}) collective-permute-start(bf16[64,2560]{1,0:T(8,128)(2,1)S(1)} %pack.1.refs_0_), channel_id=1, source_target_pairs={{0,8},{2,10},{4,12},{6,14},{8,0},{10,2},{12,4},{14,6},{16,24},{18,... | collective-permute-start | bytes 983048 | tf_op jit(solution)/shard_map/ppermute | solution.py:71
  10.1 16.4 %collective-permute-start = (bf16[64,2560]{1,0:T(8,128)(2,1)S(1)}, bf16[64,2560]{1,0:T(8,128)(2,1)S(1)}, u32[]{:S(2)}, u32[]{:S(2)}) collective-permute-start(bf16[64,2560]{1,0:T(8,128)(2,1)S(1)} %pack.1.refs_0_), channel_id=1, source_target_pairs={{0,16},{2,18},{4,20},{6,22},{8,24},{10,26},{12,28},{14,30},{16,0},... | collective-permute-start | bytes 983048 | tf_op jit(solution)/shard_map/ppermute | solution.py:71
  26.6 13.4 %collective-permute-start.6 = (bf16[128,2560]{1,0:T(8,128)(2,1)S(1)}, bf16[128,2560]{1,0:T(8,128)(2,1)S(1)}, u32[]{:S(2)}, u32[]{:S(2)}) collective-permute-start(bf16[128,2560]{1,0:T(8,128)(2,1)S(1)} %get-tuple-element.103), channel_id=1, source_target_pairs={{0,8},{2,10},{4,12},{6,14},{8,0},{10,2},{12,4},{14,6},{16,24},{18,... | collective-permute-start | bytes 1966088 | tf_op jit(solution)/shard_map/ppermute | solution.py:71
  27.2 14.2 %collective-permute-start.10 = (bf16[128,2560]{1,0:T(8,128)(2,1)S(1)}, bf16[128,2560]{1,0:T(8,128)(2,1)S(1)}, u32[]{:S(2)}, u32[]{:S(2)}) collective-permute-start(bf16[128,2560]{1,0:T(8,128)(2,1)S(1)} %get-tuple-element.104), channel_id=1, source_target_pairs={{0,2},{2,0},{4,6},{6,4},{8,10},{10,8},{12,14},{14,12},{16,18},{18,... | collective-permute-start | bytes 1966088 | tf_op jit(solution)/shard_map/ppermute | solution.py:71
  28.7 14.4 %collective-permute-start.8 = (bf16[128,2560]{1,0:T(8,128)(2,1)S(1)}, bf16[128,2560]{1,0:T(8,128)(2,1)S(1)}, u32[]{:S(2)}, u32[]{:S(2)}) collective-permute-start(bf16[128,2560]{1,0:T(8,128)(2,1)S(1)} %get-tuple-element.104), channel_id=1, source_target_pairs={{0,4},{2,6},{4,0},{6,2},{8,12},{10,14},{12,8},{14,10},{16,20},{18,... | collective-permute-start | bytes 1966088 | tf_op jit(solution)/shard_map/ppermute | solution.py:71
  31.3 29.8 %collective-permute-start.5 = (bf16[384,2560]{1,0:T(8,128)(2,1)S(1)}, bf16[384,2560]{1,0:T(8,128)(2,1)S(1)}, u32[]{:S(2)}, u32[]{:S(2)}) collective-permute-start(bf16[384,2560]{1,0:T(8,128)(2,1)S(1)} %stack.15.refs_0_), channel_id=1, source_target_pairs={{0,1},{1,0},{2,3},{3,2},{4,5},{5,4},{6,7},{7,6},{8,9},{9,8},{10,11... | collective-permute-start | bytes 5898248 | tf_op jit(solution)/shard_map/ppermute | solution.py:75
  31.8 14.0 %collective-permute-start.18 = (bf16[256,1024]{1,0:T(8,128)(2,1)S(1)}, bf16[256,1024]{1,0:T(8,128)(2,1)S(1)}, u32[]{:S(2)}, u32[]{:S(2)}) collective-permute-start(bf16[256,1024]{1,0:T(8,128)(2,1)S(1)} %norm_latents.1.refs_3_.refs_14_.refs_17_), channel_id=1, source_target_pairs={{0,1},{1,0},{2,3},{3,2},{4,5},{5,4},{6,7},{7,6},{8,9},{9,8},{10,11... | collective-permute-start | bytes 1572872 | tf_op jit(solution)/shard_map/ppermute | solution.py:75
  43.2 13.1 %collective-permute-start.12 = (bf16[64,2560]{1,0:T(8,128)(2,1)S(1)}, bf16[64,2560]{1,0:T(8,128)(2,1)S(1)}, u32[]{:S(2)}, u32[]{:S(2)}) collective-permute-start(bf16[64,2560]{1,0:T(8,128)(2,1)S(1)} %get-tuple-element.105), channel_id=1, source_target_pairs={{0,16},{2,18},{4,20},{6,22},{8,24},{10,26},{12,28},{14,30},{16,0},... | collective-permute-start | bytes 983048 | tf_op jit(solution)/shard_map/ppermute | solution.py:71
  43.8 12.9 %collective-permute-start.16 = (bf16[128,2560]{1,0:T(8,128)(2,1)S(1)}, bf16[128,2560]{1,0:T(8,128)(2,1)S(1)}, u32[]{:S(2)}, u32[]{:S(2)}) collective-permute-start(bf16[128,2560]{1,0:T(8,128)(2,1)S(1)} %get-tuple-element.107), channel_id=1, source_target_pairs={{0,2},{2,0},{4,6},{6,4},{8,10},{10,8},{12,14},{14,12},{16,18},{18,... | collective-permute-start | bytes 1966088 | tf_op jit(solution)/shard_map/ppermute | solution.py:71
  44.4 11.8 %collective-permute-start.14 = (bf16[64,2560]{1,0:T(8,128)(2,1)S(1)}, bf16[64,2560]{1,0:T(8,128)(2,1)S(1)}, u32[]{:S(2)}, u32[]{:S(2)}) collective-permute-start(bf16[64,2560]{1,0:T(8,128)(2,1)S(1)} %get-tuple-element.106), channel_id=1, source_target_pairs={{0,4},{2,6},{4,0},{6,2},{8,12},{10,14},{12,8},{14,10},{16,20},{18,... | collective-permute-start | bytes 983048 | tf_op jit(solution)/shard_map/ppermute | solution.py:71
  45.9 10.9 %collective-permute-start.7 = (bf16[128,2560]{1,0:T(8,128)(2,1)S(1)}, bf16[128,2560]{1,0:T(8,128)(2,1)S(1)}, u32[]{:S(2)}, u32[]{:S(2)}) collective-permute-start(bf16[128,2560]{1,0:T(8,128)(2,1)S(1)} %collective-permute-done.6.refs_0_.refs_2_), channel_id=1, source_target_pairs={{0,1},{1,0},{2,3},{3,2},{4,5},{5,4},{6,7},{7,6},{8,9},{9,8},{10,11... | collective-permute-start | bytes 1966088 | tf_op jit(solution)/shard_map/ppermute | solution.py:75
  56.7 4.4 %collective-permute-start.17 = (bf16[128,2560]{1,0:T(8,128)(2,1)S(1)}, bf16[128,2560]{1,0:T(8,128)(2,1)S(1)}, u32[]{:S(2)}, u32[]{:S(2)}) collective-permute-start(bf16[128,2560]{1,0:T(8,128)(2,1)S(1)} %collective-permute-done.16.refs_12_), channel_id=1, source_target_pairs={{0,1},{1,0},{2,3},{3,2},{4,5},{5,4},{6,7},{7,6},{8,9},{9,8},{10,11... | collective-permute-start | bytes 1966088 | tf_op jit(solution)/shard_map/ppermute | solution.py:75
  56.8 3.8 %collective-permute-start.13 = (bf16[64,2560]{1,0:T(8,128)(2,1)S(1)}, bf16[64,2560]{1,0:T(8,128)(2,1)S(1)}, u32[]{:S(2)}, u32[]{:S(2)}) collective-permute-start(bf16[64,2560]{1,0:T(8,128)(2,1)S(1)} %collective-permute-done.12.refs_8_), channel_id=1, source_target_pairs={{0,1},{1,0},{2,3},{3,2},{4,5},{5,4},{6,7},{7,6},{8,9},{9,8},{10,11... | collective-permute-start | bytes 983048 | tf_op jit(solution)/shard_map/ppermute | solution.py:75
  59.3 12.2 %collective-permute-start.20 = (f32[256,1024]{1,0:T(8,128)S(1)}, f32[256,1024]{1,0:T(8,128)S(1)}, u32[]{:S(2)}, u32[]{:S(2)}) collective-permute-start(f32[256,1024]{1,0:T(8,128)S(1)} %bitcast.34), channel_id=1, source_target_pairs={{0,1},{1,0},{2,3},{3,2},{4,5},{5,4},{6,7},{7,6},{8,9},{9,8},{10,11... | collective-permute-start | bytes 3145736 | tf_op jit(solution)/shard_map/ppermute | solution.py:75
  60.7 10.8 %collective-permute-start.21 = (f32[256,1024]{1,0:T(8,128)S(1)}, f32[256,1024]{1,0:T(8,128)S(1)}, u32[]{:S(2)}, u32[]{:S(2)}) collective-permute-start(f32[256,1024]{1,0:T(8,128)S(1)} %bitcast.46), channel_id=1, source_target_pairs={{0,1},{1,0},{2,3},{3,2},{4,5},{5,4},{6,7},{7,6},{8,9},{9,8},{10,11... | collective-permute-start | bytes 3145736 | tf_op jit(solution)/shard_map/ppermute | solution.py:75
  94.3 13.8 %collective-permute-start.23 = (bf16[64,1792]{1,0:T(8,128)(2,1)S(1)}, bf16[64,1792]{1,0:T(8,128)(2,1)}, u32[]{:S(2)}, u32[]{:S(2)}) collective-permute-start(bf16[64,1792]{1,0:T(8,128)(2,1)S(1)} %get-tuple-element.115), channel_id=1, source_target_pairs={{0,4},{2,6},{4,0},{6,2},{8,12},{10,14},{12,8},{14,10},{16,20},{18,... | collective-permute-start | bytes 688136 | tf_op jit(solution)/shard_map/ppermute | solution.py:71
  95.9 12.3 %collective-permute-start.24 = (bf16[64,1792]{1,0:T(8,128)(2,1)S(1)}, bf16[64,1792]{1,0:T(8,128)(2,1)}, u32[]{:S(2)}, u32[]{:S(2)}) collective-permute-start(bf16[64,1792]{1,0:T(8,128)(2,1)S(1)} %get-tuple-element.116), channel_id=1, source_target_pairs={{0,16},{2,18},{4,20},{6,22},{8,24},{10,26},{12,28},{14,30},{16,0},... | collective-permute-start | bytes 688136 | tf_op jit(solution)/shard_map/ppermute | solution.py:71
  96.1 13.5 %collective-permute-start.22 = (bf16[128,1792]{1,0:T(8,128)(2,1)S(1)}, bf16[128,1792]{1,0:T(8,128)(2,1)}, u32[]{:S(2)}, u32[]{:S(2)}) collective-permute-start(bf16[128,1792]{1,0:T(8,128)(2,1)S(1)} %get-tuple-element.114), channel_id=1, source_target_pairs={{0,2},{2,0},{4,6},{6,4},{8,10},{10,8},{12,14},{14,12},{16,18},{18,... | collective-permute-start | bytes 1376264 | tf_op jit(solution)/shard_map/ppermute | solution.py:71
  96.8 29.9 %collective-permute-start.31 = (bf16[128,1792]{1,0:T(8,128)(2,1)}, bf16[128,1792]{1,0:T(8,128)(2,1)}, u32[]{:S(2)}, u32[]{:S(2)}) collective-permute-start(bf16[128,1792]{1,0:T(8,128)(2,1)} %get-tuple-element.138), channel_id=1, source_target_pairs={{0,2},{2,0},{4,6},{6,4},{8,10},{10,8},{12,14},{14,12},{16,18},{18,... | collective-permute-start | bytes 1376264 | tf_op jit(solution)/shard_map/ppermute | solution.py:71
  110.8 17.4 %collective-permute-start.32 = (bf16[128,1792]{1,0:T(8,128)(2,1)S(1)}, bf16[128,1792]{1,0:T(8,128)(2,1)S(1)}, u32[]{:S(2)}, u32[]{:S(2)}) collective-permute-start(bf16[128,1792]{1,0:T(8,128)(2,1)S(1)} %add_convert_fusion.1), channel_id=1, source_target_pairs={{0,4},{2,6},{4,0},{6,2},{8,12},{10,14},{12,8},{14,10},{16,20},{18,... | collective-permute-start | bytes 1376264 | tf_op jit(solution)/shard_map/ppermute | solution.py:71
  112.5 15.7 %collective-permute-start.33 = (bf16[128,1792]{1,0:T(8,128)(2,1)S(1)}, bf16[128,1792]{1,0:T(8,128)(2,1)S(1)}, u32[]{:S(2)}, u32[]{:S(2)}) collective-permute-start(bf16[128,1792]{1,0:T(8,128)(2,1)S(1)} %add_convert_fusion), channel_id=1, source_target_pairs={{0,8},{2,10},{4,12},{6,14},{8,0},{10,2},{12,4},{14,6},{16,24},{18,... | collective-permute-start | bytes 1376264 | tf_op jit(solution)/shard_map/ppermute | solution.py:71
  125.1 10.3 %collective-permute-start.25 = (f32[512,384]{1,0:T(8,128)}, f32[512,384]{1,0:T(8,128)}, u32[]{:S(2)}, u32[]{:S(2)}) collective-permute-start(f32[512,384]{1,0:T(8,128)} %get-tuple-element.121.refs_14_.refs_3_), channel_id=1, source_target_pairs={{0,1},{1,0},{2,3},{3,2},{4,5},{5,4},{6,7},{7,6},{8,9},{9,8},{10,11... | collective-permute-start | bytes 2359304 | tf_op jit(solution)/shard_map/ppermute | solution.py:75
  125.2 20.2 %collective-permute-start.29 = (bf16[64,1792]{1,0:T(8,128)(2,1)S(1)}, bf16[64,1792]{1,0:T(8,128)(2,1)}, u32[]{:S(2)}, u32[]{:S(2)}) collective-permute-start(bf16[64,1792]{1,0:T(8,128)(2,1)S(1)} %copy-done.30), channel_id=1, source_target_pairs={{0,2},{2,0},{4,6},{6,4},{8,10},{10,8},{12,14},{14,12},{16,18},{18,... | collective-permute-start | bytes 688136 | tf_op jit(solution)/shard_map/ppermute | solution.py:71
  126.7 18.8 %collective-permute-start.30 = (bf16[64,1792]{1,0:T(8,128)(2,1)S(1)}, bf16[64,1792]{1,0:T(8,128)(2,1)}, u32[]{:S(2)}, u32[]{:S(2)}) collective-permute-start(bf16[64,1792]{1,0:T(8,128)(2,1)S(1)} %copy-done.28), channel_id=1, source_target_pairs={{0,4},{2,6},{4,0},{6,2},{8,12},{10,14},{12,8},{14,10},{16,20},{18,... | collective-permute-start | bytes 688136 | tf_op jit(solution)/shard_map/ppermute | solution.py:71
  132.2 13.6 %collective-permute-start.36 = (bf16[64,1792]{1,0:T(8,128)(2,1)}, bf16[64,1792]{1,0:T(8,128)(2,1)}, u32[]{:S(2)}, u32[]{:S(2)}) collective-permute-start(bf16[64,1792]{1,0:T(8,128)(2,1)} %get-tuple-element.184), channel_id=1, source_target_pairs={{0,16},{2,18},{4,20},{6,22},{8,24},{10,26},{12,28},{14,30},{16,0},... | collective-permute-start | bytes 688136 | tf_op jit(solution)/shard_map/ppermute | solution.py:71
  133.5 12.5 %collective-permute-start.34 = (bf16[64,1792]{1,0:T(8,128)(2,1)}, bf16[64,1792]{1,0:T(8,128)(2,1)}, u32[]{:S(2)}, u32[]{:S(2)}) collective-permute-start(bf16[64,1792]{1,0:T(8,128)(2,1)} %get-tuple-element.185), channel_id=1, source_target_pairs={{0,8},{2,10},{4,12},{6,14},{8,0},{10,2},{12,4},{14,6},{16,24},{18,... | collective-permute-start | bytes 688136 | tf_op jit(solution)/shard_map/ppermute | solution.py:71
  135.5 10.5 %collective-permute-start.35 = (bf16[64,1792]{1,0:T(8,128)(2,1)}, bf16[64,1792]{1,0:T(8,128)(2,1)}, u32[]{:S(2)}, u32[]{:S(2)}) collective-permute-start(bf16[64,1792]{1,0:T(8,128)(2,1)} %get-tuple-element.186), channel_id=1, source_target_pairs={{0,6},{2,4},{4,2},{6,0},{8,14},{10,12},{12,10},{14,8},{16,22},{18,... | collective-permute-start | bytes 688136 | tf_op jit(solution)/shard_map/ppermute | solution.py:71
  145.9 8.1 %collective-permute-start.37 = (bf16[128,768]{1,0:T(8,128)(2,1)}, bf16[128,768]{1,0:T(8,128)(2,1)S(1)}, u32[]{:S(2)}, u32[]{:S(2)}) collective-permute-start(bf16[128,768]{1,0:T(8,128)(2,1)} %get-tuple-element.149), channel_id=1, source_target_pairs={{0,2},{2,0},{4,6},{6,4},{8,10},{10,8},{12,14},{14,12},{16,18},{18,... | collective-permute-start | bytes 589832 | tf_op jit(solution)/shard_map/ppermute | solution.py:71
  146.6 12.9 %collective-permute-start.28 = (bf16[128,768]{1,0:T(8,128)(2,1)}, bf16[128,768]{1,0:T(8,128)(2,1)S(1)}, u32[]{:S(2)}, u32[]{:S(2)}) collective-permute-start(bf16[128,768]{1,0:T(8,128)(2,1)} %get-tuple-element.130.refs_8_), channel_id=1, source_target_pairs={{0,2},{2,0},{4,6},{6,4},{8,10},{10,8},{12,14},{14,12},{16,18},{18,... | collective-permute-start | bytes 589832 | tf_op jit(solution)/shard_map/ppermute | solution.py:71
  148.0 8.2 %collective-permute-start.40 = (bf16[64,768]{1,0:T(8,128)(2,1)}, bf16[64,768]{1,0:T(8,128)(2,1)S(1)}, u32[]{:S(2)}, u32[]{:S(2)}) collective-permute-start(bf16[64,768]{1,0:T(8,128)(2,1)} %get-tuple-element.152), channel_id=1, source_target_pairs={{0,16},{2,18},{4,20},{6,22},{8,24},{10,26},{12,28},{14,30},{16,0},... | collective-permute-start | bytes 294920 | tf_op jit(solution)/shard_map/ppermute | solution.py:71
  148.5 7.8 %collective-permute-start.41 = (bf16[64,768]{1,0:T(8,128)(2,1)}, bf16[64,768]{1,0:T(8,128)(2,1)S(1)}, u32[]{:S(2)}, u32[]{:S(2)}) collective-permute-start(bf16[64,768]{1,0:T(8,128)(2,1)} %get-tuple-element.153), channel_id=1, source_target_pairs={{0,4},{2,6},{4,0},{6,2},{8,12},{10,14},{12,8},{14,10},{16,20},{18,... | collective-permute-start | bytes 294920 | tf_op jit(solution)/shard_map/ppermute | solution.py:71
  155.0 6.7 %collective-permute-start.38 = (bf16[128,768]{1,0:T(8,128)(2,1)S(1)}, bf16[128,768]{1,0:T(8,128)(2,1)S(1)}, u32[]{:S(2)}, u32[]{:S(2)}) collective-permute-start(bf16[128,768]{1,0:T(8,128)(2,1)S(1)} %add_convert_fusion.6), channel_id=1, source_target_pairs={{0,4},{2,6},{4,0},{6,2},{8,12},{10,14},{12,8},{14,10},{16,20},{18,... | collective-permute-start | bytes 589832 | tf_op jit(solution)/shard_map/ppermute | solution.py:71
  157.2 5.7 %collective-permute-start.42 = (bf16[128,768]{1,0:T(8,128)(2,1)S(1)}, bf16[128,768]{1,0:T(8,128)(2,1)S(1)}, u32[]{:S(2)}, u32[]{:S(2)}) collective-permute-start(bf16[128,768]{1,0:T(8,128)(2,1)S(1)} %add_convert_fusion.5), channel_id=1, source_target_pairs={{0,8},{2,10},{4,12},{6,14},{8,0},{10,2},{12,4},{14,6},{16,24},{18,... | collective-permute-start | bytes 589832 | tf_op jit(solution)/shard_map/ppermute | solution.py:71
  157.4 12.1 %collective-permute-start.26 = (bf16[64,768]{1,0:T(8,128)(2,1)}, bf16[64,768]{1,0:T(8,128)(2,1)S(1)}, u32[]{:S(2)}, u32[]{:S(2)}) collective-permute-start(bf16[64,768]{1,0:T(8,128)(2,1)} %get-tuple-element.127), channel_id=1, source_target_pairs={{0,2},{2,0},{4,6},{6,4},{8,10},{10,8},{12,14},{14,12},{16,18},{18,... | collective-permute-start | bytes 294920 | tf_op jit(solution)/shard_map/ppermute | solution.py:71
  158.5 11.1 %collective-permute-start.27 = (bf16[64,768]{1,0:T(8,128)(2,1)}, bf16[64,768]{1,0:T(8,128)(2,1)S(1)}, u32[]{:S(2)}, u32[]{:S(2)}) collective-permute-start(bf16[64,768]{1,0:T(8,128)(2,1)} %get-tuple-element.128), channel_id=1, source_target_pairs={{0,4},{2,6},{4,0},{6,2},{8,12},{10,14},{12,8},{14,10},{16,20},{18,... | collective-permute-start | bytes 294920 | tf_op jit(solution)/shard_map/ppermute | solution.py:71
  164.1 5.5 %collective-permute-start.39 = (bf16[64,768]{1,0:T(8,128)(2,1)S(1)}, bf16[64,768]{1,0:T(8,128)(2,1)S(1)}, u32[]{:S(2)}, u32[]{:S(2)}) collective-permute-start(bf16[64,768]{1,0:T(8,128)(2,1)S(1)} %get-tuple-element.189), channel_id=1, source_target_pairs={{0,8},{2,10},{4,12},{6,14},{8,0},{10,2},{12,4},{14,6},{16,24},{18,... | collective-permute-start | bytes 294920 | tf_op jit(solution)/shard_map/ppermute | solution.py:71
  164.2 5.6 %collective-permute-start.44 = (bf16[64,768]{1,0:T(8,128)(2,1)S(1)}, bf16[64,768]{1,0:T(8,128)(2,1)S(1)}, u32[]{:S(2)}, u32[]{:S(2)}) collective-permute-start(bf16[64,768]{1,0:T(8,128)(2,1)S(1)} %get-tuple-element.190), channel_id=1, source_target_pairs={{0,16},{2,18},{4,20},{6,22},{8,24},{10,26},{12,28},{14,30},{16,0},... | collective-permute-start | bytes 294920 | tf_op jit(solution)/shard_map/ppermute | solution.py:71
  166.0 5.5 %collective-permute-start.43 = (bf16[64,768]{1,0:T(8,128)(2,1)S(1)}, bf16[64,768]{1,0:T(8,128)(2,1)S(1)}, u32[]{:S(2)}, u32[]{:S(2)}) collective-permute-start(bf16[64,768]{1,0:T(8,128)(2,1)S(1)} %get-tuple-element.191), channel_id=1, source_target_pairs={{0,6},{2,4},{4,2},{6,0},{8,14},{10,12},{12,10},{14,8},{16,22},{18,... | collective-permute-start | bytes 294920 | tf_op jit(solution)/shard_map/ppermute | solution.py:71
  169.5 3.6 %collective-permute-start.46 = (f32[64,1792]{1,0:T(8,128)S(1)}, f32[64,1792]{1,0:T(8,128)S(1)}, u32[]{:S(2)}, u32[]{:S(2)}) collective-permute-start(f32[64,1792]{1,0:T(8,128)S(1)} %convert_add_fusion.refs_3_), channel_id=1, source_target_pairs={{0,1},{1,0},{2,3},{3,2},{4,5},{5,4},{6,7},{7,6},{8,9},{9,8},{10,11... | collective-permute-start | bytes 1376264 | tf_op jit(solution)/shard_map/ppermute | solution.py:75
  178.2 4.8 %collective-permute-start.50 = (f32[8,1024]{1,0:T(8,128)S(1)}, f32[8,1024]{1,0:T(8,128)S(1)}, u32[]{:S(2)}, u32[]{:S(2)}) collective-permute-start(f32[8,1024]{1,0:T(8,128)S(1)} %get-tuple-element.167), channel_id=1, source_target_pairs={{0,6},{2,4},{4,2},{6,0},{8,14},{10,12},{12,10},{14,8},{16,22},{18,... | collective-permute-start | bytes 98312 | tf_op jit(solution)/shard_map/ppermute | solution.py:71
  180.3 3.9 %collective-permute-start.49 = (f32[8,1024]{1,0:T(8,128)S(1)}, f32[8,1024]{1,0:T(8,128)S(1)}, u32[]{:S(2)}, u32[]{:S(2)}) collective-permute-start(f32[8,1024]{1,0:T(8,128)S(1)} %get-tuple-element.167), channel_id=1, source_target_pairs={{0,4},{2,6},{4,0},{6,2},{8,12},{10,14},{12,8},{14,10},{16,20},{18,... | collective-permute-start | bytes 98312 | tf_op jit(solution)/shard_map/ppermute | solution.py:71
  180.8 3.9 %collective-permute-start.48 = (f32[8,1024]{1,0:T(8,128)S(1)}, f32[8,1024]{1,0:T(8,128)S(1)}, u32[]{:S(2)}, u32[]{:S(2)}) collective-permute-start(f32[8,1024]{1,0:T(8,128)S(1)} %get-tuple-element.167), channel_id=1, source_target_pairs={{0,2},{2,0},{4,6},{6,4},{8,10},{10,8},{12,14},{14,12},{16,18},{18,... | collective-permute-start | bytes 98312 | tf_op jit(solution)/shard_map/ppermute | solution.py:71
  184.7 5.8 %collective-permute-start.53 = (f32[8,1024]{1,0:T(8,128)S(1)}, f32[8,1024]{1,0:T(8,128)S(1)}, u32[]{:S(2)}, u32[]{:S(2)}) collective-permute-start(f32[8,1024]{1,0:T(8,128)S(1)} %add_add_fusion.1), channel_id=1, source_target_pairs={{0,24},{2,26},{4,28},{6,30},{8,16},{10,18},{12,20},{14,22},{16,8},... | collective-permute-start | bytes 98312 | tf_op jit(solution)/shard_map/ppermute | solution.py:71
  187.2 4.8 %collective-permute-start.52 = (f32[8,1024]{1,0:T(8,128)S(1)}, f32[8,1024]{1,0:T(8,128)S(1)}, u32[]{:S(2)}, u32[]{:S(2)}) collective-permute-start(f32[8,1024]{1,0:T(8,128)S(1)} %add_add_fusion.1), channel_id=1, source_target_pairs={{0,16},{2,18},{4,20},{6,22},{8,24},{10,26},{12,28},{14,30},{16,0},... | collective-permute-start | bytes 98312 | tf_op jit(solution)/shard_map/ppermute | solution.py:71
  187.2 4.8 %collective-permute-start.51 = (f32[8,1024]{1,0:T(8,128)S(1)}, f32[8,1024]{1,0:T(8,128)S(1)}, u32[]{:S(2)}, u32[]{:S(2)}) collective-permute-start(f32[8,1024]{1,0:T(8,128)S(1)} %add_add_fusion.1), channel_id=1, source_target_pairs={{0,8},{2,10},{4,12},{6,14},{8,0},{10,2},{12,4},{14,6},{16,24},{18,... | collective-permute-start | bytes 98312 | tf_op jit(solution)/shard_map/ppermute | solution.py:71
  (68 other events, 1008.9 us)
